TPU v7x, 32 devices: a whole 2x2x4 slice. The times are simulated.
32 devices in a mesh: dp: 8 (over z, x), fsdp: 4 (over y, core).
Axes of the slice: x: 2, y: 2, z: 4, core: 2. Of those that a mesh axis runs over, the one named last changes fastest.
Arguments:
- hidden_in: bfloat16 [8, 2048, 1024], P('dp', 'fsdp'), may hold values from -6 to 6
- params: bfloat16 [12591104], P(('dp', 'fsdp'))
- cotangent: bfloat16 [8, 2048, 1024], P('dp', 'fsdp'), may hold values from -6 to 6
- source_ids: int32 [8], P('dp'), may hold values from 0 to 15
- corpus_weight: float32 [16], replicated, may hold values from 0.3 to 3
- positions: int32 [8, 2048], P('dp', 'fsdp'), may hold values from 0 to 2047, as said below
Outputs:
- output: bfloat16 [8, 2048, 1024], P('dp', 'fsdp')
- input_grad: bfloat16 [8, 2048, 1024], P('dp', 'fsdp')
- param_grads: float32 [12591104], P(('dp', 'fsdp'))
- statistics: float32 [2], replicated
Inputs may be any that keep to these rules, and one draw needn't show every extreme that they name: Each row is a pack of documents: a row begins at position 0, positions rise by one along the row and fall back to 0 where a new document starts; some row is a single document.
All inputs are finite; a program needn't handle non-finite values.
Results may differ from a plain program's by a relative error of at most 0.015.
Values may be sent and summed in bfloat16 or wider, within the bound.
A program may use at most 256 MiB of HBM per device.

v0:
```python
import math

import jax
import jax.numpy as jnp
from jax import lax
from jax.sharding import PartitionSpec as P

D = 1024
HEADS = 16
HEAD_DIM = 64
FF = 4096


EPSILON = 1e-05
MASKED = -1e30


def unpack(flat_params):
    end_qkv = 3 * D * D
    end_out = end_qkv + D * D
    end_up = end_out + D * FF
    end_down = end_up + FF * D
    return (
        flat_params[:end_qkv].reshape(D, 3 * D),
        flat_params[end_qkv:end_out].reshape(D, D),
        flat_params[end_out:end_up].reshape(D, FF),
        flat_params[end_up:end_down].reshape(FF, D),
        flat_params[end_down:].reshape(8, D).astype(jnp.float32),
    )


def norm_forward(values, gain_row, shift_row):
    center = values - jnp.mean(values, axis=-1, keepdims=True)
    spread = jnp.mean(center * center, axis=-1, keepdims=True)
    inverse = lax.rsqrt(spread + EPSILON)
    unit_rows = center * inverse
    return (unit_rows * gain_row + shift_row, unit_rows, inverse)


def norm_backward(grad_rows, unit_rows, inverse, gain_row):
    scaled = grad_rows * gain_row
    first_mean = jnp.mean(scaled, axis=-1, keepdims=True)
    second_mean = jnp.mean(scaled * unit_rows, axis=-1, keepdims=True)
    into_values = inverse * (scaled - first_mean - unit_rows * second_mean)
    gain_grad = jnp.sum(grad_rows * unit_rows, axis=(0, 1))
    shift_grad = jnp.sum(grad_rows, axis=(0, 1))
    return (into_values, gain_grad, shift_grad)


def rotate(values, cosine, sine_table):
    half_dim = HEAD_DIM // 2
    front_half = values[..., :half_dim]
    back_half = values[..., half_dim:]
    return jnp.concatenate(
        [
            front_half * cosine - back_half * sine_table,
            back_half * cosine + front_half * sine_table,
        ],
        axis=-1,
    )


def unrotate(grad_rows, cosine, sine_table):
    half_dim = HEAD_DIM // 2
    front_half = grad_rows[..., :half_dim]
    back_half = grad_rows[..., half_dim:]
    return jnp.concatenate(
        [
            front_half * cosine + back_half * sine_table,
            back_half * cosine - front_half * sine_table,
        ],
        axis=-1,
    )


def fetch_forward(shard_part):
    whole = lax.all_gather(shard_part, ("dp", "fsdp"), axis=0, tiled=True)
    return whole


def fetch_backward(shard_part):
    whole = lax.all_gather(shard_part, ("dp", "fsdp"), axis=0, tiled=True)
    return whole


def reduce_grads(flat_grads):
    owned = lax.psum_scatter(flat_grads, ("dp", "fsdp"), scatter_dimension=0, tiled=True)
    return owned


def scores_for(query_group, key_group, query_first, key_first):
    raw_scores = jnp.einsum(
        "rqhd,rkhd->rhqk", query_group, key_group, preferred_element_type=jnp.float32
    )
    query_index = query_first + jnp.arange(query_group.shape[1], dtype=jnp.int32)
    key_index = key_first + jnp.arange(key_group.shape[1], dtype=jnp.int32)
    allowed = key_index[None, :] <= query_index[:, None]
    return jnp.where(allowed[None, None], raw_scores * (1.0 / math.sqrt(HEAD_DIM)), MASKED)


def block_of(array, number, width, dim):
    return lax.dynamic_slice_in_dim(array, number * width, width, dim)


def per_device(hidden_in, params, cotangent, source_ids, corpus_weight, positions):
    rows_here = hidden_in.shape[0]
    tokens_here = hidden_in.shape[1]
    group_size = min(4, HEADS)
    group_width = group_size * HEAD_DIM
    score_scale = 1.0 / math.sqrt(HEAD_DIM)
    half_dim = HEAD_DIM // 2
    bfloat = jnp.bfloat16
    single = jnp.float32
    place = lax.axis_index("fsdp")
    own_first = place * tokens_here
    gathered = fetch_forward(params)
    w_qkv, w_out, w_up, w_down, norm_rows = unpack(gathered)
    frequency = jnp.exp(jnp.arange(half_dim, dtype=single) * (-2.0 * math.log(10000.0) / HEAD_DIM))
    angles = positions.astype(single)[:, :, None] * frequency
    cosine = jnp.cos(angles)[:, :, None, :]
    sine_table = jnp.sin(angles)[:, :, None, :]
    shape_heads = (rows_here, tokens_here, HEADS, HEAD_DIM)
    inputs = hidden_in.astype(single)
    normed, normed_unit, normed_inverse = norm_forward(inputs, norm_rows[0], norm_rows[1])
    normed_low = normed.astype(bfloat)
    mixed_rows = jnp.einsum("rtd,de->rte", normed_low, w_qkv, preferred_element_type=single)
    queries = rotate(mixed_rows[..., :D].reshape(shape_heads), cosine, sine_table).astype(bfloat)
    key_rows = rotate(mixed_rows[..., D : 2 * D].reshape(shape_heads), cosine, sine_table)
    key_rows = key_rows.reshape(rows_here, tokens_here, D).astype(bfloat)
    value_rows = mixed_rows[..., 2 * D :].astype(bfloat)
    all_keys, all_values = (
        lax.all_gather(key_rows, "fsdp", axis=1, tiled=True),
        lax.all_gather(value_rows, "fsdp", axis=1, tiled=True),
    )
    length = all_keys.shape[1]

    def columns(array, head_group):
        picked = array[..., head_group * group_width : (head_group + 1) * group_width]
        return picked.reshape(array.shape[0], array.shape[1], group_size, HEAD_DIM)

    def heads_of(array, head_group):
        return array[:, :, head_group * group_size : (head_group + 1) * group_size]

    stat_shape = (rows_here, group_size, tokens_here, 1)
    pieces = []
    log_totals = []
    for head_group in range(HEADS // group_size):
        query_group = heads_of(queries, head_group)
        key_group = columns(all_keys, head_group)
        value_group = columns(all_values, head_group)

        def peak_step(number, carry, query_group=query_group, key_group=key_group):
            peak, total = carry
            scores = scores_for(
                query_group,
                block_of(key_group, number, tokens_here, 1),
                own_first,
                number * tokens_here,
            )
            new_peak = jnp.maximum(peak, jnp.max(scores, axis=-1, keepdims=True))
            total = total * jnp.exp(peak - new_peak) + jnp.sum(
                jnp.exp(scores - new_peak), axis=-1, keepdims=True
            )
            return (new_peak, total)

        peak, total = lax.fori_loop(
            0,
            place + 1,
            peak_step,
            (jnp.full(stat_shape, MASKED, single), jnp.zeros(stat_shape, single)),
        )
        log_total = peak + jnp.log(total)
        log_totals.append(log_total)

        def value_step(
            number,
            summed,
            query_group=query_group,
            key_group=key_group,
            value_group=value_group,
            log_total=log_total,
        ):
            scores = scores_for(
                query_group,
                block_of(key_group, number, tokens_here, 1),
                own_first,
                number * tokens_here,
            )
            weights = jnp.exp(scores - log_total).astype(bfloat)
            return summed + jnp.einsum(
                "rhqk,rkhd->rqhd",
                weights,
                block_of(value_group, number, tokens_here, 1),
                preferred_element_type=single,
            )

        pieces.append(
            lax.fori_loop(
                0,
                place + 1,
                value_step,
                jnp.zeros((rows_here, tokens_here, group_size, HEAD_DIM), single),
            )
        )
    attended = jnp.concatenate(pieces, axis=2).reshape(rows_here, tokens_here, D).astype(bfloat)
    branch = jnp.einsum("rtd,de->rte", attended, w_out, preferred_element_type=single)
    branch_norm, branch_unit, branch_inverse = norm_forward(branch, norm_rows[2], norm_rows[3])
    residual = inputs + branch_norm
    entered, entered_unit, entered_inverse = norm_forward(residual, norm_rows[4], norm_rows[5])
    entered_low = entered.astype(bfloat)
    lifted = jnp.einsum("rtd,df->rtf", entered_low, w_up, preferred_element_type=single)
    activated = jax.nn.gelu(lifted).astype(bfloat)
    lowered = jnp.einsum("rtf,fd->rtd", activated, w_down, preferred_element_type=single)
    lowered_norm, lowered_unit, lowered_inverse = norm_forward(lowered, norm_rows[6], norm_rows[7])
    output = (residual + lowered_norm).astype(bfloat)
    local_squares = jnp.stack([jnp.mean(branch * branch), jnp.mean(lowered * lowered)])
    statistics = lax.psum(local_squares, ("dp", "fsdp")) / lax.axis_size(("dp", "fsdp"))
    source_table = jnp.arange(corpus_weight.shape[0], dtype=jnp.int32)
    row_scale = jnp.sum(
        jnp.where(source_ids[:, None] == source_table[None, :], corpus_weight[None, :], 0.0), axis=1
    )
    upstream = cotangent.astype(single) * row_scale[:, None, None]
    gathered_back = fetch_backward(params)
    w_qkv, w_out, w_up, w_down, norm_rows = unpack(gathered_back)
    back_keys, back_values = (
        lax.all_gather(key_rows, "fsdp", axis=1, tiled=True),
        lax.all_gather(value_rows, "fsdp", axis=1, tiled=True),
    )
    lowered_grad, out_mlp_gain, out_mlp_shift = norm_backward(
        upstream, lowered_unit, lowered_inverse, norm_rows[6]
    )
    lowered_grad_low = lowered_grad.astype(bfloat)
    grad_down = jnp.einsum(
        "rtf,rtd->fd", activated, lowered_grad_low, preferred_element_type=single
    )
    activated_grad = jnp.einsum(
        "rtd,fd->rtf", lowered_grad_low, w_down, preferred_element_type=single
    )
    lifted_grad = jax.vjp(jax.nn.gelu, lifted)[1](activated_grad)[0].astype(bfloat)
    grad_up = jnp.einsum("rtd,rtf->df", entered_low, lifted_grad, preferred_element_type=single)
    entered_grad = jnp.einsum("rtf,df->rtd", lifted_grad, w_up, preferred_element_type=single)
    into_residual, in_mlp_gain, in_mlp_shift = norm_backward(
        entered_grad, entered_unit, entered_inverse, norm_rows[4]
    )
    residual_grad = upstream + into_residual
    branch_grad, out_attn_gain, out_attn_shift = norm_backward(
        residual_grad, branch_unit, branch_inverse, norm_rows[2]
    )
    branch_grad_low = branch_grad.astype(bfloat)
    grad_out = jnp.einsum("rtd,rte->de", attended, branch_grad_low, preferred_element_type=single)
    attended_grad = jnp.einsum(
        "rte,de->rtd", branch_grad_low, w_out, preferred_element_type=single
    ).astype(bfloat)
    group_shape = (rows_here, tokens_here, group_size, HEAD_DIM)
    full_shape = (rows_here, length, group_size, HEAD_DIM)
    query_grads = []
    key_grads = []
    value_grads = []
    dot_list = []
    for head_group in range(HEADS // group_size):
        query_group = heads_of(queries, head_group)
        key_group = columns(back_keys, head_group)
        value_group = columns(back_values, head_group)
        grad_group = columns(attended_grad, head_group)
        log_total = log_totals[head_group]

        def dot_step(
            number,
            dots,
            query_group=query_group,
            key_group=key_group,
            value_group=value_group,
            grad_group=grad_group,
            log_total=log_total,
        ):
            scores = scores_for(
                query_group,
                block_of(key_group, number, tokens_here, 1),
                own_first,
                number * tokens_here,
            )
            probabilities = jnp.exp(scores - log_total)
            prob_grad = jnp.einsum(
                "rqhd,rkhd->rhqk",
                grad_group,
                block_of(value_group, number, tokens_here, 1),
                preferred_element_type=single,
            )
            return dots + jnp.sum(prob_grad * probabilities, axis=-1, keepdims=True)

        dot_rows = lax.fori_loop(0, place + 1, dot_step, jnp.zeros(stat_shape, single))
        dot_list.append(dot_rows)

        def grad_step(
            number,
            carry,
            query_group=query_group,
            key_group=key_group,
            value_group=value_group,
            grad_group=grad_group,
            log_total=log_total,
            dot_rows=dot_rows,
        ):
            query_sum, key_sum, value_sum = carry
            key_block = block_of(key_group, number, tokens_here, 1)
            scores = scores_for(query_group, key_block, own_first, number * tokens_here)
            probabilities = jnp.exp(scores - log_total)
            probabilities_low = probabilities.astype(bfloat)
            prob_grad = jnp.einsum(
                "rqhd,rkhd->rhqk",
                grad_group,
                block_of(value_group, number, tokens_here, 1),
                preferred_element_type=single,
            )
            score_grad = (probabilities * (prob_grad - dot_rows)).astype(bfloat)
            query_sum = (
                query_sum
                + jnp.einsum(
                    "rhqk,rkhd->rqhd", score_grad, key_block, preferred_element_type=single
                )
                * score_scale
            )
            key_part = (
                jnp.einsum(
                    "rhqk,rqhd->rkhd", score_grad, query_group, preferred_element_type=single
                )
                * score_scale
            )
            value_part = jnp.einsum(
                "rhqk,rqhd->rkhd", probabilities_low, grad_group, preferred_element_type=single
            )
            key_sum = lax.dynamic_update_slice_in_dim(
                key_sum,
                block_of(key_sum, number, tokens_here, 1) + key_part,
                number * tokens_here,
                1,
            )
            value_sum = lax.dynamic_update_slice_in_dim(
                value_sum,
                block_of(value_sum, number, tokens_here, 1) + value_part,
                number * tokens_here,
                1,
            )
            return (query_sum, key_sum, value_sum)

        start = (
            jnp.zeros(group_shape, single),
            jnp.zeros(full_shape, single),
            jnp.zeros(full_shape, single),
        )
        query_sum, key_sum, value_sum = lax.fori_loop(0, place + 1, grad_step, start)
        query_grads.append(query_sum)
        key_grads.append(key_sum)
        value_grads.append(value_sum)
    query_grad = jnp.concatenate(query_grads, axis=2)
    key_full = jnp.concatenate(key_grads, axis=2).reshape(rows_here, length, D)
    value_full = jnp.concatenate(value_grads, axis=2).reshape(rows_here, length, D)
    key_grad, value_grad = (
        lax.psum_scatter(
            key_full.astype(jnp.bfloat16), "fsdp", scatter_dimension=1, tiled=True
        ).astype(jnp.float32),
        lax.psum_scatter(
            value_full.astype(jnp.bfloat16), "fsdp", scatter_dimension=1, tiled=True
        ).astype(jnp.float32),
    )
    query_plain = unrotate(query_grad, cosine, sine_table).reshape(rows_here, tokens_here, D)
    key_plain = unrotate(key_grad.reshape(shape_heads), cosine, sine_table).reshape(
        rows_here, tokens_here, D
    )
    mixed_grad = jnp.concatenate([query_plain, key_plain, value_grad], axis=-1).astype(bfloat)
    grad_qkv = jnp.einsum("rtd,rte->de", normed_low, mixed_grad, preferred_element_type=single)
    normed_grad = jnp.einsum("rte,de->rtd", mixed_grad, w_qkv, preferred_element_type=single)
    into_input, in_attn_gain, in_attn_shift = norm_backward(
        normed_grad, normed_unit, normed_inverse, norm_rows[0]
    )
    input_grad = (residual_grad + into_input).astype(bfloat)
    norm_grads = jnp.stack(
        [
            in_attn_gain,
            in_attn_shift,
            out_attn_gain,
            out_attn_shift,
            in_mlp_gain,
            in_mlp_shift,
            out_mlp_gain,
            out_mlp_shift,
        ]
    )
    flat_grads = jnp.concatenate(
        [
            grad_qkv.reshape(-1),
            grad_out.reshape(-1),
            grad_up.reshape(-1),
            grad_down.reshape(-1),
            norm_grads.reshape(-1),
        ]
    )
    param_grads = reduce_grads(flat_grads)
    return (output, input_grad, param_grads, statistics)


def solution(mesh):
    in_specs = (
        P("dp", "fsdp", None),
        P(("dp", "fsdp")),
        P("dp", "fsdp", None),
        P("dp"),
        P(),
        P("dp", "fsdp"),
    )
    out_specs = (P("dp", "fsdp", None), P("dp", "fsdp", None), P(("dp", "fsdp")), P())
    return jax.shard_map(
        per_device, mesh=mesh, in_specs=in_specs, out_specs=out_specs, check_vma=False
    )
```

profile of v0, /device:TPU:5, one launch (start us, length us, event | category | flops | bytes accessed | tf_op | source)
XLA Modules:
  0.0 1915.1 jit_solution(1215356906285420291)
XLA Ops:
  7.2 9.1 reshape.1670
  17.1 276.7 %all-gather.9.cloned.1.call-done = bf16[32,1,393472]{2,1,0:T(2,128)(2,1)} async-done(((bf16[1,1,393472]{2,1,0:T(2,128)(2,1)}), bf16[32,1,393472]{2,1,0:T(2,128)(2,1)}) %all-gather.9.cloned.1.call-update) | async-done | bytes 25182224 | tf_op jit(solution)/shard_map/all_gather | solution.py:77
  293.8 149.4 %reduce.54 = bf16[32,393472]{1,0:T(8,128)(2,1)} reduce(bf16[32,1,393472]{2,1,0:T(2,128)(2,1)} %all-gather.9.cloned.1.call-done, bf16[]{:T(256)} %constant.285), dimensions={1}, to_apply=%all-gather.reduce_sub_computation | reduce | bytes 50364416 | tf_op jit(solution)/shard_map/all_gather | solution.py:77
  443.2 59.1 %reshape.1671 = bf16[12591104]{0:T(1024)(128)(2,1)} reshape(bf16[32,393472]{1,0:T(8,128)(2,1)} %reduce.54) | data formatting | bytes 50364416
  503.0 6.4 slice.234
  510.0 10.3 reshape.1643
  520.4 16.8 convolution_bitcast_fusion.2
  542.8 4.9 fusion.362
  556.2 11.5 fusion.361
  567.7 13.3 slice.220
  581.0 13.6 slice.218
  597.1 4.0 fusion.364
  602.5 6.3 all-gather.7.cloned.1.call-done
  608.8 4.0 fusion.363
  612.8 12.3 while.190
  626.0 15.6 while.191
  626.2 3.7 fusion.514
  630.1 3.7 fusion.514
  634.0 3.7 fusion.514
  637.9 3.7 fusion.514
  643.8 12.3 while.188
  657.0 15.6 while.189
  657.3 3.7 fusion.509
  661.2 3.7 fusion.509
  665.1 3.7 fusion.509
  669.0 3.7 fusion.509
  675.1 8.5 while.186
  684.5 15.8 while.187
  685.1 3.6 fusion.504
  689.0 3.6 fusion.504
  692.8 3.6 fusion.504
  696.7 3.6 fusion.504
  703.0 8.5 while.184
  712.5 15.5 while.185
  712.7 3.7 fusion.499
  716.7 3.6 fusion.499
  720.5 3.6 fusion.499
  724.3 3.6 fusion.499
  734.0 8.3 fusion.349
  742.3 5.3 fusion.368
  752.3 16.1 fusion.302
  768.4 9.5 fusion.318
  778.7 3.6 fusion.322
  787.1 10.3 while.198
  801.3 35.7 %while.199 = (s32[]{:T(128)}, f32[1,512,4,64]{1,3,2,0:T(8,128)S(1)}, f32[1,2048,4,64]{1,3,2,0:T(8,128)}, f32[1,2048,4,64]{1,3,2,0:T(8,128)}, s32[]{:T(128)}, /*i...) while((s32[]{:T(128)}, f32[1,512,4,64]{1,3,2,0:T(8,128)S(1)}, ...), condition=%wide.region_58.59_spmd, body=%wide.region_57.58_spmd.sunk | while | flops 682492928 | bytes 25723140 | solution.py:351
  838.4 17.8 while.196
  859.4 46.8 %while.197 = (s32[]{:T(128)}, f32[1,512,4,64]{1,3,2,0:T(8,128)S(1)}, f32[1,2048,4,64]{1,3,2,0:T(8,128)}, f32[1,2048,4,64]{1,3,2,0:T(8,128)}, s32[]{:T(128)}, /*i...) while((s32[]{:T(128)}, f32[1,512,4,64]{1,3,2,0:T(8,128)S(1)}, ...), condition=%wide.region_53.54_spmd, body=%wide.region_52.53_spmd.sunk | while | flops 682492928 | bytes 24674536 | solution.py:351
  907.0 14.0 while.194
  924.3 39.5 %while.195 = (s32[]{:T(128)}, f32[1,512,4,64]{1,3,2,0:T(8,128)S(1)}, f32[1,2048,4,64]{1,3,2,0:T(8,128)}, f32[1,2048,4,64]{1,3,2,0:T(8,128)}, s32[]{:T(128)}, /*i...) while((s32[]{:T(128)}, f32[1,512,4,64]{1,3,2,0:T(8,128)S(1)}, ...), condition=%wide.region_48.49_spmd, body=%wide.region_47.48_spmd.sunk | while | flops 682492928 | bytes 25723140 | solution.py:351
  964.0 14.0 while.192
  981.3 39.0 %while.193 = (s32[]{:T(128)}, f32[1,512,4,64]{1,3,2,0:T(8,128)S(1)}, f32[1,2048,4,64]{1,3,2,0:T(8,128)}, f32[1,2048,4,64]{1,3,2,0:T(8,128)}, s32[]{:T(128)}, /*i...) while((s32[]{:T(128)}, f32[1,512,4,64]{1,3,2,0:T(8,128)S(1)}, ...), condition=%wide.region_43.44_spmd, body=%wide.region_42.43_spmd.sunk | while | flops 682492928 | bytes 24674536 | solution.py:351
  1041.2 4.9 convolution_bitcast_fusion.1
  1046.2 7.2 copy.179
  1053.5 10.5 convolution_bitcast_fusion
  1063.9 8.5 copy.180
  1079.9 37.7 %reduce-scatter.5.cloned.1.call-done = bf16[1,512,1024]{1,2,0:T(8,128)(2,1)} async-done(((bf16[1,2048,1024]{1,2,0:T(8,128)(2,1)}), bf16[1,512,1024]{1,2,0:T(8,128)(2,1)}) %reduce-scatter.5.cloned.1.call-update) | async-done | bytes 1048592 | tf_op jit(solution)/shard_map/reduce_scatter | solution.py:362
  1117.6 7.2 fusion.316
  1124.9 9.8 convolution_bitcast_fusion.3
  1135.0 12.1 copy.177
  1147.1 11.2 constant_dynamic-update-slice_fusion.4
  1163.9 8.4 constant_dynamic-update-slice_fusion.6
  1174.5 6.1 constant_dynamic-update-slice_fusion.5
  1182.9 42.2 %psum.7 = f32[2]{0:T(128)S(1)} all-reduce(f32[2]{0:T(128)S(1)} %pad_maximum_fusion.9), channel_id=1, replica_groups=mesh['dp'=8,'fsdp'=4] {'dp','fsdp'}, use_global_device_ids=true, to_apply=%region_74.75 | all-reduce | flops 2 | bytes 16 | tf_op jit(solution)/shard_map/psum | solution.py:217
  1228.9 676.2 %all-reduce.3.cloned.1.call-done = f32[12591104]{0:T(1024)} async-done(((f32[12591104]{0:T(1024)}), f32[12591104]{0:T(1024)}) %all-reduce.3.cloned.1.call-update) | async-done | bytes 50364432
  (694 shorter events, 365.4 us)
Async XLA Ops:
  7.2 9.3 copy-start.23
  7.2 286.6 %all-gather.9.cloned.1.call-start = ((), (), s32[]{:S(2)}) async-start(), calls=%async_computation.6 | async-start | bytes 51938304 | tf_op jit(solution)/shard_map/all_gather | solution.py:77
  16.4 580.7 %all-gather.5.cloned.1.call-start = ((), (), s32[]{:S(2)}) async-start(), calls=%async_computation.2 | async-start | bytes 5242880 | tf_op jit(solution)/shard_map/all_gather | solution.py:133
  16.7 503.7 %copy-start.59 = (f32[512]{0:T(512)}, f32[512]{0:T(512)S(1)}, u32[]{:S(2)}) copy-start(f32[512]{0:T(512)S(1)} %broadcast_multiply_fusion.11) | copy-start | bytes 6148
  17.1 503.2 %copy-start.71 = (f32[512]{0:T(512)}, f32[512]{0:T(512)S(1)}, u32[]{:S(2)}) copy-start(f32[512]{0:T(512)S(1)} %add_rsqrt_fusion.3) | copy-start | bytes 6148
  510.0 10.3 copy-start.57
  510.0 10.3 copy-start.83
  510.0 223.9 %copy-start.85 = (f32[1024]{0:T(1024)}, f32[1024]{0:T(1024)S(1)}, u32[]{:S(2)}) copy-start(f32[1024]{0:T(1024)S(1)} %get-tuple-element.1526) | copy-start | bytes 12292
  510.0 268.7 %copy-start.55 = (f32[1024]{0:T(1024)}, f32[1024]{0:T(1024)S(1)}, u32[]{:S(2)}) copy-start(f32[1024]{0:T(1024)S(1)} %get-tuple-element.1527) | copy-start | bytes 12292
  520.4 20.7 %copy-start.88 = (s32[1,512]{1,0:T(1,128)S(1)}, s32[1,512]{1,0:T(1,128)}, u32[]{:S(2)}) copy-start(s32[1,512]{1,0:T(1,128)} %param.43) | copy-start | bytes 6148
  520.4 21.4 %copy-start.94 = (f32[16]{0:T(128)S(1)}, f32[16]{0:T(128)}, u32[]{:S(2)}) copy-start(f32[16]{0:T(128)} %param.42) | copy-start | bytes 196
  541.0 67.7 %all-gather.7.cloned.1.call-start = ((), (), s32[]{:S(2)}) async-start(), calls=%async_computation.3 | async-start | bytes 5242880 | tf_op jit(solution)/shard_map/all_gather | solution.py:132
  542.8 10.1 copy-start.45
  542.8 10.1 copy-start.47
  556.2 519.7 %reduce-scatter.3.cloned.1.call-start = ((), (), s32[]{:S(2)}) async-start(), calls=%async_computation.4 | async-start | bytes 5242880 | tf_op jit(solution)/shard_map/reduce_scatter | solution.py:359
  581.0 13.7 slice-start
  712.5 15.5 copy-start.38
  712.5 15.5 copy-start.39
  712.5 15.5 copy-start.40
  732.8 9.4 slice-start.9
  733.6 45.2 %copy-start.11 = (f32[1,512,1024]{2,1,0:T(8,128)}, f32[1,512,1024]{2,1,0:T(8,128)S(1)}, u32[]{:S(2)}) copy-start(f32[1,512,1024]{2,1,0:T(8,128)S(1)} %get-tuple-element.1450) | copy-start | bytes 6291460
  733.6 45.2 %copy-start.63 = (f32[512]{0:T(512)}, f32[512]{0:T(512)S(1)}, u32[]{:S(2)}) copy-start(f32[512]{0:T(512)S(1)} %broadcast_multiply_fusion.9) | copy-start | bytes 6148
  733.9 44.8 %copy-start.73 = (f32[512]{0:T(512)}, f32[512]{0:T(512)S(1)}, u32[]{:S(2)}) copy-start(f32[512]{0:T(512)S(1)} %add_rsqrt_fusion.1) | copy-start | bytes 6148
  734.0 8.3 slice-start.10
  748.9 19.5 %copy-start.75 = (f32[512]{0:T(512)}, f32[512]{0:T(512)S(1)}, u32[]{:S(2)}) copy-start(f32[512]{0:T(512)S(1)} %add_rsqrt_fusion) | copy-start | bytes 6148
  752.3 16.1 copy-start.89
  752.3 16.1 copy-start.91
  801.3 37.0 %copy-start.5 = (bf16[1,512,4,64]{1,3,2,0:T(8,128)(2,1)S(1)}, bf16[1,512,4,64]{1,3,2,0:T(8,128)(2,1)}, u32[]{:S(2)}) copy-start(bf16[1,512,4,64]{1,3,2,0:T(8,128)(2,1)} %copy-done.4) | copy-start | bytes 786436
  801.3 37.0 %copy-start.82 = (f32[1,4,512,1]{2,1,3,0:T(4,128)S(1)}, f32[1,4,512,1]{2,1,3,0:T(4,128)}, u32[]{:S(2)}) copy-start(f32[1,4,512,1]{2,1,3,0:T(4,128)} %copy-done.81) | copy-start | bytes 24580
  859.4 46.8 %copy-start.44 = (bf16[1,512,256]{2,1,0:T(8,128)(2,1)S(1)}, bf16[1,512,256]{2,1,0:T(8,128)(2,1)}, u32[]{:S(2)}) copy-start(bf16[1,512,256]{2,1,0:T(8,128)(2,1)} %get-tuple-element.1515) | copy-start | bytes 786436
  859.4 47.0 %copy-start.3 = (bf16[1,512,4,64]{1,3,2,0:T(8,128)(2,1)S(1)}, bf16[1,512,4,64]{1,3,2,0:T(8,128)(2,1)}, u32[]{:S(2)}) copy-start(bf16[1,512,4,64]{1,3,2,0:T(8,128)(2,1)} %copy-done.2) | copy-start | bytes 786436
  859.4 47.0 %copy-start.9 = (bf16[1,2048,4,64]{1,3,2,0:T(8,128)(2,1)S(1)}, bf16[1,2048,4,64]{1,3,2,0:T(8,128)(2,1)}, u32[]{:S(2)}) copy-start(bf16[1,2048,4,64]{1,3,2,0:T(8,128)(2,1)} %copy-done.8) | copy-start | bytes 3145732
  859.4 47.0 %copy-start.80 = (f32[1,4,512,1]{2,1,3,0:T(4,128)S(1)}, f32[1,4,512,1]{2,1,3,0:T(4,128)}, u32[]{:S(2)}) copy-start(f32[1,4,512,1]{2,1,3,0:T(4,128)} %copy-done.79) | copy-start | bytes 24580
  924.3 39.5 %copy-start.43 = (bf16[1,512,256]{2,1,0:T(8,128)(2,1)S(1)}, bf16[1,512,256]{2,1,0:T(8,128)(2,1)}, u32[]{:S(2)}) copy-start(bf16[1,512,256]{2,1,0:T(8,128)(2,1)} %get-tuple-element.1512) | copy-start | bytes 786436
  924.3 39.7 %copy-start.1 = (bf16[1,512,4,64]{1,3,2,0:T(8,128)(2,1)S(1)}, bf16[1,512,4,64]{1,3,2,0:T(8,128)(2,1)}, u32[]{:S(2)}) copy-start(bf16[1,512,4,64]{1,3,2,0:T(8,128)(2,1)} %copy-done) | copy-start | bytes 786436
  924.3 39.7 %copy-start.7 = (bf16[1,2048,4,64]{1,3,2,0:T(8,128)(2,1)S(1)}, bf16[1,2048,4,64]{1,3,2,0:T(8,128)(2,1)}, u32[]{:S(2)}) copy-start(bf16[1,2048,4,64]{1,3,2,0:T(8,128)(2,1)} %copy-done.6) | copy-start | bytes 3145732
  924.3 39.7 %copy-start.78 = (f32[1,4,512,1]{2,1,3,0:T(4,128)S(1)}, f32[1,4,512,1]{2,1,3,0:T(4,128)}, u32[]{:S(2)}) copy-start(f32[1,4,512,1]{2,1,3,0:T(4,128)} %copy-done.77) | copy-start | bytes 24580
  1026.2 91.4 %reduce-scatter.5.cloned.1.call-start = ((), (), s32[]{:S(2)}) async-start(), calls=%async_computation.5 | async-start | bytes 5242880 | tf_op jit(solution)/shard_map/reduce_scatter | solution.py:362
  1032.9 872.2 %all-reduce.3.cloned.1.call-start = ((), (), s32[]{:S(2)}) async-start(), calls=%async_computation.7 | async-start | bytes 100728832
  1046.1 7.3 copy-start.31
  1046.1 7.3 copy-start.37
  1046.1 7.3 copy-start.54
  1046.1 7.3 copy-start.62
  1046.1 7.3 copy-start.76
  1046.2 7.3 copy-start.90
  1046.2 7.3 copy-start.92
  1063.9 10.2 copy-start.16
  1063.9 11.1 copy-start.14
  1077.4 40.2 %copy-start.25 = (bf16[1,512,1024]{2,1,0:T(8,128)(2,1)S(1)}, bf16[1,512,1024]{2,1,0:T(8,128)(2,1)}, u32[]{:S(2)}) copy-start(bf16[1,512,1024]{2,1,0:T(8,128)(2,1)} %param.38) | copy-start | bytes 3145732
  1077.4 40.2 %copy-start.58 = (f32[1024]{0:T(1024)S(1)}, f32[1024]{0:T(1024)}, u32[]{:S(2)}) copy-start(f32[1024]{0:T(1024)} %copy-done.57) | copy-start | bytes 12292
  1077.4 40.2 %copy-start.60 = (f32[512]{0:T(512)S(1)}, f32[512]{0:T(512)}, u32[]{:S(2)}) copy-start(f32[512]{0:T(512)} %copy-done.59) | copy-start | bytes 6148
  1077.4 40.2 %copy-start.72 = (f32[512]{0:T(512)S(1)}, f32[512]{0:T(512)}, u32[]{:S(2)}) copy-start(f32[512]{0:T(512)} %copy-done.71) | copy-start | bytes 6148
  1117.6 7.2 copy-start.84
  1117.6 7.2 copy-start.93
  1124.8 9.8 copy-start.32
  1147.1 11.2 copy-start.22
  1147.1 13.6 slice-start.1
  1147.1 13.6 slice-start.2
  1147.1 15.4 slice-start.3
  1158.3 14.0 slice-start.5
  1163.9 8.4 slice-start.6
  1163.9 8.7 slice-start.7
  1163.9 10.5 slice-start.8
  1181.4 44.2 %copy-start.21 = (f32[1,512,1024]{2,1,0:T(8,128)S(1)}, f32[1,512,1024]{2,1,0:T(8,128)}, u32[]{:S(2)}) copy-start(f32[1,512,1024]{2,1,0:T(8,128)} %copy-done.20) | copy-start | bytes 6291460
  (56 other events, 187.1 us)
Sparse Core Ops, SparseCore 0:
  16.5 277.2 all-gather.8
  541.1 31.4 all-gather.4
  574.2 34.4 all-gather.6
  1026.4 44.1 reduce-scatter.2
  1073.0 44.5 reduce-scatter.4
  1181.5 723.5 all-reduce.2
where the time goes:
time: 1920 us
  waiting for transfers between devices  997 us (52%)
  matrix products  382 us (20%)
  local copies, waits for them, and re-layouts  255 us (13%)
  other arithmetic  217 us (11%)
  blocking collectives  42.2 us (2%)
    unnamed x7, waiting for transfers between devices  676 us
    all_gather x1, waiting for transfers between devices, fetch_forward(): whole = lax.all_gather(shard_part, ('dp', 'fsdp'), axis=0, tiled=True)  277 us
    all_gather x1, other arithmetic, fetch_forward(): whole = lax.all_gather(shard_part, ('dp', 'fsdp'), axis=0, tiled=True)  149 us
    unnamed x224, local copies, waits for them, and re-layouts  149 us
    dot_general x16, matrix products, value_step(): jnp.einsum('rhqk,rkhd->rqhd', weights, block_of(value_group, number, toke...  58.3 us
    dot_general x48, matrix products, scores_for(): jnp.einsum('rqhd,rkhd->rhqk', query_group, key_group, preferred_element_t...  54.1 us
    dot_general x16, matrix products, grad_step(): jnp.einsum('rhqk,rqhd->rkhd', probabilities_low, grad_group, preferred_el...  49.9 us
    dot_general x16, matrix products, grad_step(): jnp.einsum('rhqk,rqhd->rkhd', score_grad, query_group, preferred_element_...  42.5 us
  transfers between devices with their start and end apart: 6, of which 4 were waited for; matrix products, arithmetic and copies ran while one was open for 6% of the time, Pallas kernels for 0%

commit v1 on v0

v1 whole, which is shorter than its diff:
```python
import functools
import math

import jax
import jax.numpy as jnp
from jax import lax
from jax.experimental import pallas as pl
from jax.experimental.pallas import tpu as pltpu
from jax.sharding import PartitionSpec as P

D = 1024
HEADS = 16
HEAD_DIM = 64
FF = 4096
EPSILON = 1e-05
MASKED = -1e30
SCALE = 1.0 / math.sqrt(HEAD_DIM)
LOG2E = 1.4426950408889634

MESH = pl.DeviceIdType.MESH
bf = jnp.bfloat16
f32 = jnp.float32
SHARD = 384
NATURAL = 3074
MIB = 2**20

VM = pl.BlockSpec(memory_space=pltpu.VMEM)
ANY = pl.BlockSpec(memory_space=pl.ANY)
DMA = pltpu.SemaphoreType.DMA


def params_for(collective=None, mib=48):
    if collective is None:
        return pltpu.CompilerParams(vmem_limit_bytes=mib * MIB)
    return pltpu.CompilerParams(
        collective_id=collective, has_side_effects=True, vmem_limit_bytes=mib * MIB
    )


def coords():
    dp, fs = lax.axis_index("dp"), lax.axis_index("fsdp")
    return dp // 2, lax.rem(dp, 2), fs // 2, lax.rem(fs, 2)


def dev(z, x, y, c):
    return (z * 2 + x, y * 2 + c)


def linear(i):
    return (i // 4, lax.rem(i, 4))


def remote(src, dst, send, recv, to):
    return pltpu.make_async_remote_copy(
        src_ref=src, dst_ref=dst, send_sem=send, recv_sem=recv, device_id=to, device_id_type=MESH
    )


def greet(bar, device):
    pl.semaphore_signal(bar, inc=1, device_id=device, device_id_type=MESH)


def meet_neighbours(z, x, y, c, plane, more=0):
    bar = pltpu.get_barrier_semaphore()
    for device in plane:
        greet(bar, device)

    @pl.when(z < 3)
    def _():
        greet(bar, dev(z + 1, x, y, c))

    @pl.when(z > 0)
    def _():
        greet(bar, dev(z - 1, x, y, c))

    line = jnp.where(z < 3, 1, 0) + jnp.where(z > 0, 1, 0)
    pl.semaphore_wait(bar, len(plane) + line + more)


def add_rows(dst, *srcs):
    total = srcs[0][...].astype(f32)
    for part in srcs[1:]:
        total = total + part[...].astype(f32)
    dst[...] = total.astype(dst.dtype)


def add_tiles(dst, rows, *srcs):
    for at in range(0, rows, 16):
        add_rows(dst.at[at : at + 16], *[part.at[at : at + 16] for part in srcs])


def first_kernel(
    p_ref, h_ref, pos_ref,
    hid_ref, wq_ref, can_ref, nrm_ref, posall_ref,
    ext, tail, units, us, ur, hs, hr, ns, nr, ps, pr, ls,
):
    z, x, y, c = coords()
    xn, yn, cn = 1 - x, 1 - y, 1 - c
    s = (z * 2 + x) * 4 + y * 2 + c
    f = y * 2 + c
    nxt, prv = lax.rem(s + 1, 32), lax.rem(s + 31, 32)
    core = dev(z, x, y, cn)
    xs, xo, ys, yo = dev(z, xn, y, c), dev(z, xn, y, cn), dev(z, x, yn, c), dev(z, x, yn, cn)
    bar = pltpu.get_barrier_semaphore()
    greet(bar, linear(nxt))
    greet(bar, linear(prv))

    @pl.when(s != 31)
    def _():
        greet(bar, (7, 3))

    ext[64 : 64 + NATURAL, :] = p_ref[...].astype(f32)
    tail[...] = ext[NATURAL : NATURAL + 64, :]
    more = 2 + jnp.where(s == 31, 31, 0)
    meet_neighbours(z, x, y, c, [core, xs, xo, ys, yo], more)

    halves, half = 2, 256

    def hidden_rows(owner, k):
        return hid_ref.at[pl.ds(pl.multiple_of(owner * 512 + k * half, 16), half)]

    def hidden_own(k):
        return h_ref.at[pl.ds(k * half, half)]

    over_y, over_core, over_both = yn * 2 + c, y * 2 + cn, yn * 2 + cn
    halo = remote(tail, ext.at[0:64], ns.at[0], nr.at[0], linear(nxt))
    halo.start()
    sent = []
    for k in range(halves):
        sent.append(remote(hidden_own(k), hidden_rows(f, k), hs.at[0, k], hr.at[0, k], ys))
        sent.append(remote(hidden_own(k), hidden_rows(f, k), hs.at[1, k], hr.at[1, k], core))
    for i, to in enumerate([core, ys, yo]):
        sent.append(remote(pos_ref, posall_ref.at[f], ps.at[i], pr.at[i], to))
    for copy in sent:
        copy.start()
    own = [
        pltpu.make_async_copy(
            h_ref, hid_ref.at[pl.ds(pl.multiple_of(f * 512, 512), 512)], ls.at[0]
        ),
        pltpu.make_async_copy(pos_ref, posall_ref.at[f], ls.at[1]),
    ]
    for copy in own:
        copy.start()
    halo.wait()
    base = 64 - 2 * s

    def lines(first, count, apart, k):
        return ext[pl.ds(base + 8 * first + k, count, stride=8 * apart), :].astype(bf)

    def order(to, first, count, apart):
        for j in range(apart):
            for k in range(8):
                can_ref[to + j * count : to + (j + 1) * count, 128 * k : 128 * k + 128] = lines(
                    first + j, count, apart, k
                )

    @pl.when(z == 0)
    def _():
        for j in range(3):
            for k in range(8):
                at = 128 * (k % 2)
                units[k // 2, j, :, at : at + 128] = lines(j, 128, 3, k)
        can_ref[...] = jnp.zeros_like(can_ref)

    @pl.when((s == 8) | (s == 9) | (s >= 22))
    def _():
        order(0, 0, 384, 1)

    @pl.when(s == 10)
    def _():
        order(0, 0, 256, 1)
        order(256, 256, 32, 4)

    @pl.when((s >= 11) & (s <= 20))
    def _():
        order(0, 0, 96, 4)

    @pl.when(s == 21)
    def _():
        order(0, 0, 32, 4)
        order(128, 128, 256, 1)

    def norm_send(i):
        return remote(nrm_ref, nrm_ref, ns.at[1 + i], nr.at[1], linear(i))

    @pl.when(s == 31)
    def _():
        for k in range(8):
            nrm_ref[:, 128 * k : 128 * k + 128] = ext[pl.ds(base + 8 * 384 + k, 8, stride=8), :]

        def go(i, _):
            norm_send(i).start()
            return 0

        lax.fori_loop(0, 31, go, 0)

    slots = [yn * 2 + c, yn * 2 + cn, y * 2 + cn, y * 2 + c]

    def target(xx, yy, cc):
        at = pl.multiple_of((xx * 4 + yy * 2 + cc) * 128, 128)
        return wq_ref.at[:, pl.ds(at, 128)]

    def up(q):
        unit = units.at[slots[q]]
        return remote(unit, unit, us.at[0, q], ur.at[0, q], dev(z + 1, x, y, c))

    def arrive(ref, sem):
        remote(ref, ref, us.at[0, 0], sem, core).wait_recv()

    mine = target(x, y, c)
    for q in range(4):
        unit = units.at[slots[q]]

        @pl.when(z > 0)
        def _():
            arrive(unit, ur.at[0, q])

        @pl.when(z < 3)
        def _():
            up(q).start()

        if q == 0:
            out = [remote(unit, mine, us.at[1, 0], ur.at[1, 0], ys)]
        elif q == 1:
            out = [remote(unit, mine, us.at[1, 1], ur.at[1, 1], yo)]
        elif q == 2:
            out = [
                remote(unit, mine, us.at[1, 2], ur.at[1, 2], xo),
                remote(unit, mine, us.at[1, 3], ur.at[1, 3], core),
            ]
        else:
            out = [remote(unit, mine, us.at[2, 0], ur.at[2, 0], xs)]
            copy = pltpu.make_async_copy(unit, mine, ls.at[2])
            copy.start()
            own.append(copy)
        for copy in out:
            copy.start()
        sent += out
    for i, cc in enumerate((c, cn)):
        ref = target(x, yn, cc)
        arrive(ref, ur.at[1, i])
        copy = remote(ref, ref, us.at[2, 1 + i], ur.at[2, 1 + i], xs)
        copy.start()
        sent.append(copy)
    for k in range(halves):
        ref = hidden_rows(over_y, k)
        arrive(ref, hr.at[0, k])
        copy = remote(ref, ref, hs.at[2, k], hr.at[2, k], core)
        copy.start()
        sent.append(copy)
    arrive(target(xn, y, cn), ur.at[1, 2])
    arrive(target(x, y, cn), ur.at[1, 3])
    arrive(target(xn, y, c), ur.at[2, 0])
    arrive(target(xn, yn, c), ur.at[2, 1])
    arrive(target(xn, yn, cn), ur.at[2, 2])
    for k in range(halves):
        arrive(hidden_rows(over_core, k), hr.at[1, k])
        arrive(hidden_rows(over_both, k), hr.at[2, k])
    for i, owner in enumerate([over_core, over_y, over_both]):
        arrive(posall_ref.at[owner], pr.at[i])
    for copy in sent:
        copy.wait_send()

    @pl.when(z < 3)
    def _():
        for q in range(4):
            up(q).wait_send()

    for copy in own:
        copy.wait()

    @pl.when(s == 31)
    def _():
        def go(i, _):
            norm_send(i).wait_send()
            return 0

        lax.fori_loop(0, 31, go, 0)

    @pl.when(s != 31)
    def _():
        arrive(nrm_ref, nr.at[1])


def first_gather(share, hidden, places):
    shape = jax.ShapeDtypeStruct
    return pl.pallas_call(
        first_kernel,
        out_shape=(
            shape((2048, D), bf),
            shape((3, D, 256), bf),
            shape((SHARD, D), bf),
            shape((8, D), f32),
            shape((4, 8, 128), f32),
        ),
        in_specs=[VM, VM, VM],
        out_specs=(ANY, ANY, VM, VM, VM),
        scratch_shapes=[
            pltpu.VMEM((64 + NATURAL + 6, 128), f32),
            pltpu.VMEM((64, 128), f32),
            pltpu.VMEM((4, 3, 128, 256), bf),
            DMA((3, 4)), DMA((3, 4)), DMA((3, 2)), DMA((3, 2)),
            DMA((32,)), DMA((2,)), DMA((3,)), DMA((3,)), DMA((3,)),
        ],
        compiler_params=params_for(0, 32),
    )(share, hidden, places)


CHUNKS = 4
CHUNK = SHARD // CHUNKS
UNITS = 3 * CHUNKS
OVER_X = 48


def gather_kernel(c_ref, g_ref, ss, rs, ls):
    z, x, y, c = coords()
    xn, yn, cn = 1 - x, 1 - y, 1 - c
    to_x, to_y, to_core = dev(z, xn, y, c), dev(z, x, yn, c), dev(z, x, y, cn)
    lag, core_lag = 2, 4

    def rows(zz, xx, yy, cc, k, low=0, count=CHUNK):
        s = (zz * 2 + xx) * 4 + yy * 2 + cc - 8
        return g_ref.at[pl.ds(pl.multiple_of(s * SHARD + k * CHUNK + low, 16), count)]

    local = pltpu.make_async_copy(c_ref, rows(jnp.maximum(z, 1), x, y, c, 0, 0, SHARD), ls)

    @pl.when(z >= 1)
    def _():
        local.start()

    meet_neighbours(z, x, y, c, [to_x, to_y, to_core])

    @pl.when(z >= 1)
    def _():
        local.wait()

    ZU, ZD, XO, YO, CO, XD, YD, CX, CY, CXD, CYD = range(11)

    def unit(i):
        r = i // CHUNKS
        k = i - r * CHUNKS
        first = jnp.maximum(z, 1)
        second = jnp.where(z == 2, 1, 2)
        third = jnp.where(z <= 2, 3, 1)
        zz = jnp.where(r == 0, first, jnp.where(r == 1, second, third))
        return zz, k, (zz - 1) * CHUNKS + k

    def send(kind, i):
        zz, k, q = unit(i)
        ref, to = {
            ZU: lambda: (rows(zz, x, y, c, k), dev(z + 1, x, y, c)),
            ZD: lambda: (rows(zz, x, y, c, k), dev(z - 1, x, y, c)),
            XO: lambda: (rows(zz, x, y, c, k), to_x),
            YO: lambda: (rows(zz, x, y, c, k), to_y),
            CO: lambda: (rows(zz, x, y, c, k), to_core),
            YD: lambda: (rows(zz, xn, y, c, k, OVER_X, CHUNK - OVER_X), to_y),
            XD: lambda: (rows(zz, x, yn, c, k, 0, OVER_X), to_x),
            CX: lambda: (rows(zz, xn, y, c, k), to_core),
            CY: lambda: (rows(zz, x, yn, c, k), to_core),
            CXD: lambda: (rows(zz, xn, yn, c, k, 0, OVER_X), to_core),
            CYD: lambda: (rows(zz, xn, yn, c, k, OVER_X, CHUNK - OVER_X), to_core),
        }[kind]()
        return remote(ref, ref, ss.at[kind, q], rs.at[kind, q], to)

    def arrive(kind, i):
        zz, k, q = unit(i)
        ref = {
            ZU: lambda: rows(zz, x, y, c, k),
            ZD: lambda: rows(zz, x, y, c, k),
            XO: lambda: rows(zz, xn, y, c, k),
            YO: lambda: rows(zz, x, yn, c, k),
            XD: lambda: rows(zz, xn, yn, c, k, 0, OVER_X),
            YD: lambda: rows(zz, xn, yn, c, k, OVER_X, CHUNK - OVER_X),
            CO: lambda: rows(zz, x, y, cn, k),
            CX: lambda: rows(zz, xn, y, cn, k),
            CY: lambda: rows(zz, x, yn, cn, k),
            CXD: lambda: rows(zz, xn, yn, cn, k, 0, OVER_X),
            CYD: lambda: rows(zz, xn, yn, cn, k, OVER_X, CHUNK - OVER_X),
        }[kind]()
        remote(ref, ref, ss.at[kind, q], rs.at[kind, q], to_core).wait_recv()

    def step(i, _):
        @pl.when(i < UNITS)
        def _():
            zz, _, _ = unit(i)

            @pl.when(zz < z)
            def _():
                arrive(ZU, i)

            @pl.when(zz > z)
            def _():
                arrive(ZD, i)

            @pl.when((zz <= z) & (z < 3))
            def _():
                send(ZU, i).start()

            @pl.when((zz >= z) & (z > 0))
            def _():
                send(ZD, i).start()

            for kind in (XO, YO, CO):
                send(kind, i).start()

        j = i - lag

        @pl.when((j >= 0) & (j < UNITS))
        def _():
            arrive(XO, j)
            send(YD, j).start()
            send(CX, j).start()
            arrive(YO, j)
            send(XD, j).start()
            send(CY, j).start()

        m = i - core_lag

        @pl.when(m >= 0)
        def _():
            arrive(XD, m)
            send(CXD, m).start()
            arrive(YD, m)
            send(CYD, m).start()

        return 0

    lax.fori_loop(0, UNITS + core_lag, step, 0)

    def finish(i, _):
        zz, _, _ = unit(i)
        for kind in (CO, CX, CY, CXD, CYD):
            arrive(kind, i)
        for kind in (XO, YO, CO, YD, XD, CX, CY, CXD, CYD):
            send(kind, i).wait_send()

        @pl.when((zz <= z) & (z < 3))
        def _():
            send(ZU, i).wait_send()

        @pl.when((zz >= z) & (z > 0))
        def _():
            send(ZD, i).wait_send()

        return 0

    lax.fori_loop(0, UNITS, finish, 0)


def gather_others(canonical):
    return pl.pallas_call(
        gather_kernel,
        out_shape=jax.ShapeDtypeStruct((24 * SHARD, D), bf),
        in_specs=[VM],
        out_specs=ANY,
        scratch_shapes=[DMA((11, UNITS)), DMA((11, UNITS)), DMA],
        compiler_params=params_for(1, 16),
    )(canonical)


def reduce_kernel(
    g_ref, o_ref, lb, cb, xb, yb, dxb, dyb, zub, zdb, ss, rs, cs, cr, ls
):
    z, x, y, c = coords()
    xn, yn, cn = 1 - x, 1 - y, 1 - c
    to_x, to_y, to_core = dev(z, xn, y, c), dev(z, x, yn, c), dev(z, x, y, cn)
    lag1, lag2, lag3, lag4 = 1, 2, 3, 4
    XS, YS, DXS, DYS, ZD, ZU = range(6)

    def unit(i):
        r = i // CHUNKS
        return 3 - r, i - r * CHUNKS

    def rows(zz, xx, yy, cc, k):
        s = (zz * 2 + xx) * 4 + yy * 2 + cc - 8
        return g_ref.at[pl.ds(pl.multiple_of(s * SHARD + k * CHUNK, 16), CHUNK)]

    places = [(xn, yn), (xn, y), (x, yn), (x, y)]

    def load(i, p):
        zz, k = unit(i)
        xx, yy = places[p]
        return pltpu.make_async_copy(rows(zz, xx, yy, c, k), lb.at[i, p], ls.at[i, p])

    def to_sibling(i, p):
        zz, k = unit(i)
        xx, yy = places[p]
        return remote(rows(zz, xx, yy, cn, k), cb.at[i, p], cs.at[i, p], cr.at[i, p], to_core)

    def load_all(i, _):
        for p in range(4):
            load(i, p).start()
        return 0

    lax.fori_loop(0, UNITS, load_all, 0)
    meet_neighbours(z, x, y, c, [to_x, to_y, to_core])

    def send_all(i, _):
        for p in range(4):
            to_sibling(i, p).start()
        return 0

    lax.fori_loop(0, UNITS, send_all, 0)

    def over(kind, src, dst, i, to):
        return remote(src, dst, ss.at[kind, i], rs.at[kind, i], to)

    def diag_x(i):
        return over(DXS, lb.at[i, 0, 0:OVER_X], dxb.at[i], i, to_x)

    def diag_y(i):
        return over(DYS, lb.at[i, 0, OVER_X:CHUNK], dyb.at[i], i, to_y)

    def whole_x(i):
        return over(XS, lb.at[i, 1], xb.at[i], i, to_x)

    def whole_y(i):
        return over(YS, lb.at[i, 2], yb.at[i], i, to_y)

    def down(i):
        return over(ZD, lb.at[i, 3], zub.at[i], i, dev(z - 1, x, y, c))

    def up(i):
        return over(ZU, lb.at[i, 3], zdb.at[i], i, dev(z + 1, x, y, c))

    def have(i, p):
        load(i, p).wait()
        to_sibling(i, p).wait_recv()

    def step(i, _):
        @pl.when(i < UNITS)
        def _():
            have(i, 0)
            add_tiles(lb.at[i, 0], CHUNK, lb.at[i, 0], cb.at[i, 0])
            diag_x(i).start()
            diag_y(i).start()

        j = i - lag1

        @pl.when((j >= 0) & (j < UNITS))
        def _():
            have(j, 1)
            have(j, 2)
            diag_y(j).wait_recv()
            diag_x(j).wait_recv()
            a, b = lb.at[j, 1], cb.at[j, 1]
            low, high = slice(0, OVER_X), slice(OVER_X, CHUNK)
            add_tiles(a.at[low], OVER_X, a.at[low], b.at[low])
            add_tiles(a.at[high], CHUNK - OVER_X, a.at[high], b.at[high], dyb.at[j])
            whole_x(j).start()
            a, b = lb.at[j, 2], cb.at[j, 2]
            add_tiles(a.at[low], OVER_X, a.at[low], b.at[low], dxb.at[j])
            add_tiles(a.at[high], CHUNK - OVER_X, a.at[high], b.at[high])
            whole_y(j).start()

        m = i - lag2

        @pl.when((m >= 0) & (m < UNITS))
        def _():
            zz, k = unit(m)
            have(m, 3)
            whole_x(m).wait_recv()
            whole_y(m).wait_recv()
            parts = [lb.at[m, 3], cb.at[m, 3], xb.at[m], yb.at[m]]

            @pl.when(z != zz)
            def _():
                add_tiles(lb.at[m, 3], CHUNK, *parts)

            @pl.when((z == 3) & (zz < 3))
            def _():
                down(m).start()

            @pl.when(z == 0)
            def _():
                up(m).start()

            @pl.when(z == zz)
            def _():
                add_tiles(o_ref.at[pl.ds(pl.multiple_of(k * CHUNK, 16), CHUNK)], CHUNK, *parts)

        n = i - lag3

        @pl.when((n >= 0) & (n < UNITS))
        def _():
            zz, _ = unit(n)

            @pl.when((z > zz) & (z < 3))
            def _():
                down(n).wait_recv()
                add_tiles(lb.at[n, 3], CHUNK, lb.at[n, 3], zub.at[n])
                down(n).start()

            @pl.when((z < zz) & (z > 0))
            def _():
                up(n).wait_recv()
                add_tiles(lb.at[n, 3], CHUNK, lb.at[n, 3], zdb.at[n])
                up(n).start()

        o = i - lag4

        @pl.when(o >= 0)
        def _():
            zz, k = unit(o)

            @pl.when(z == zz)
            def _():
                dst = o_ref.at[pl.ds(pl.multiple_of(k * CHUNK, 16), CHUNK)]

                @pl.when(z < 3)
                def _():
                    down(o).wait_recv()
                    add_tiles(dst, CHUNK, dst, zub.at[o])

                up(o).wait_recv()
                add_tiles(dst, CHUNK, dst, zdb.at[o])

        return 0

    lax.fori_loop(0, UNITS + lag4, step, 0)

    def finish(i, _):
        zz, _ = unit(i)
        for p in range(4):
            to_sibling(i, p).wait_send()
        for copy in (diag_x(i), diag_y(i), whole_x(i), whole_y(i)):
            copy.wait_send()

        @pl.when(z > zz)
        def _():
            down(i).wait_send()

        @pl.when(z < zz)
        def _():
            up(i).wait_send()

        return 0

    lax.fori_loop(0, UNITS, finish, 0)


def reduce_others(grads):
    def room(*shape):
        return pltpu.VMEM(shape + (D,), bf)

    return pl.pallas_call(
        reduce_kernel,
        out_shape=jax.ShapeDtypeStruct((SHARD, D), f32),
        in_specs=[ANY],
        out_specs=VM,
        scratch_shapes=[
            room(UNITS, 4, CHUNK), room(UNITS, 4, CHUNK),
            room(UNITS, CHUNK), room(UNITS, CHUNK),
            room(UNITS, OVER_X), room(UNITS, CHUNK - OVER_X),
            room(UNITS, CHUNK), room(UNITS, CHUNK),
            DMA((6, UNITS)), DMA((6, UNITS)), DMA((UNITS, 4)), DMA((UNITS, 4)), DMA((UNITS, 4)),
        ],
        compiler_params=params_for(2),
    )(grads)


def last_kernel(
    v_ref, n_ref, can_ref, nrm_ref, st_ref,
    out_ref, ng_ref, sto_ref,
    ext, hal, hsend, av, bv, cv, dv, zv, sums, sv, nc, ny, nsv, nland, sland,
    s1, r1, s2, r2, zs, zr, ms, mr, qs, qr, hsem,
):
    z, x, y, c = coords()
    xn, yn, cn = 1 - x, 1 - y, 1 - c
    s = (z * 2 + x) * 4 + y * 2 + c
    core = dev(z, x, y, cn)
    xs, xo, ys, yo = dev(z, xn, y, c), dev(z, xn, y, cn), dev(z, x, yn, c), dev(z, x, yn, cn)
    prv = lax.rem(s + 31, 32)
    bar = pltpu.get_barrier_semaphore()

    def hello(i, _):
        greet(bar, linear(lax.rem(s + i, 32)))
        return 0

    lax.fori_loop(1, 32, hello, 0)
    pl.semaphore_wait(bar, 31)
    half = 256

    def unit(xx, yy, cc):
        at = pl.multiple_of((xx * 4 + yy * 2 + cc) * 128, 128)
        return v_ref.at[:, pl.ds(at, 128), :]

    def rows(yy, cc, k):
        return n_ref.at[pl.ds(pl.multiple_of((yy * 2 + cc) * 512 + k * half, half), half)]

    far = [remote(rows(yn, cn, k), nc.at[1, k], s2.at[0, k], r2.at[0, k], core) for k in range(2)]
    near = [remote(rows(y, cn, k), nc.at[0, k], s2.at[1, k], r2.at[1, k], core) for k in range(2)]
    opposite = [
        remote(unit(xn, yn, cc), av.at[i], s1.at[i], r1.at[i], xs) for i, cc in enumerate((c, cn))
    ]
    beside = [
        remote(unit(xn, y, c), bv.at[0], s1.at[2], r1.at[2], xs),
        remote(unit(xn, y, cn), bv.at[1], s1.at[3], r1.at[3], xo),
    ]
    sibling = remote(unit(x, y, cn), cv, s1.at[4], r1.at[4], core)
    for copy in far + opposite + beside + [sibling] + near:
        copy.start()

    def tell(i):
        return remote(st_ref, sland.at[s], qs.at[i], qr.at[s], linear(lax.rem(s + i, 32)))

    def tell_all(i, _):
        tell(i).start()
        return 0

    lax.fori_loop(1, 32, tell_all, 0)
    norm_send = remote(nrm_ref, nland.at[s], ms.at[0], mr.at[s], (7, 3))

    @pl.when(s != 31)
    def _():
        norm_send.start()

    later = []
    across = []
    for i, cc in enumerate((c, cn)):
        opposite[i].wait_recv()
        for j in range(3):
            add_rows(sv.at[i, j], unit(x, yn, cc).at[j], av.at[i, j])
        copy = remote(sv.at[i], dv.at[i], s1.at[5 + i], r1.at[5 + i], (ys, yo)[i])
        copy.start()
        across.append(copy)
    for k in range(2):
        far[k].wait_recv()

        def add_far(q, _):
            at = pl.ds(pl.multiple_of(q * 32, 32), 32)
            add_rows(nsv.at[k, at], rows(yn, c, k).at[at], nc.at[1, k, at])
            return 0

        lax.fori_loop(0, half // 32, add_far, 0)
        copy = remote(nsv.at[k], ny.at[k], s2.at[2, k], r2.at[2, k], ys)
        copy.start()
        later.append(copy)

    blocks = [y * 2 + c, y * 2 + cn, yn * 2 + c, yn * 2 + cn]

    def down(q):
        return remote(sums.at[q], zv.at[q], zs.at[q], zr.at[q], dev(z - 1, x, y, c))

    for q in range(4):
        if q == 0:
            beside[0].wait_recv()
            parts = [unit(x, y, c), bv.at[0]]
        elif q == 1:
            sibling.wait_recv()
            beside[1].wait_recv()
            parts = [cv, bv.at[1]]
        else:
            across[q - 2].wait_recv()
            parts = [dv.at[q - 2]]

        @pl.when(z < 3)
        def _():
            remote(sums.at[q], zv.at[q], zs.at[q], zr.at[q], core).wait_recv()

        @pl.when(z == 3)
        def _():
            for j in range(3):
                add_rows(sums.at[q, j], *[part.at[j] for part in parts])
            down(q).start()

        @pl.when((z == 1) | (z == 2))
        def _():
            for j in range(3):
                add_rows(sums.at[q, j], zv.at[q, j], *[part.at[j] for part in parts])
            down(q).start()

        @pl.when(z == 0)
        def _():
            for j in range(3):
                total = zv[q, j].astype(f32)
                for part in parts:
                    total = total + part[j].astype(f32)
                for h in range(2):
                    at = 64 - 2 * s + 8 * j + 2 * blocks[q] + h
                    ext[pl.ds(at, 128, stride=24), :] = total[:, 128 * h : 128 * h + 128]

    base = 64 - 2 * s

    def place(src, first, count, apart):
        for j in range(apart):
            for k in range(8):
                ext[pl.ds(base + 8 * (first + j) + k, count, stride=8 * apart), :] = can_ref[
                    src + j * count : src + (j + 1) * count, 128 * k : 128 * k + 128
                ]

    @pl.when((s == 8) | (s == 9) | (s >= 22))
    def _():
        place(0, 0, 384, 1)

    @pl.when(s == 10)
    def _():
        place(0, 0, 256, 1)
        place(256, 256, 32, 4)

    @pl.when((s >= 11) & (s <= 20))
    def _():
        place(0, 0, 96, 4)

    @pl.when(s == 21)
    def _():
        place(0, 0, 32, 4)
        place(128, 128, 256, 1)

    hsend[...] = ext[0:64, :]
    halo = remote(hsend, hal, hsem.at[0], hsem.at[1], linear(prv))
    halo.start()
    for k in range(2):
        near[k].wait_recv()
        later[k].wait_recv()

        def add_own(q, _):
            at = pl.ds(pl.multiple_of(q * 32, 32), 32)
            to = pl.ds(pl.multiple_of(k * half + q * 32, 32), 32)
            add_rows(ng_ref.at[to], rows(y, c, k).at[at], nc.at[0, k, at], ny.at[k, at])
            return 0

        lax.fori_loop(0, half // 32, add_own, 0)

    def hear(i, _):
        o = lax.rem(s + i, 32)
        remote(st_ref, sland.at[o], qs.at[0], qr.at[o], core).wait_recv()
        return 0

    lax.fori_loop(1, 32, hear, 0)
    sland[pl.ds(s, 1)] = st_ref[...].reshape(1, 8, 128)
    sto_ref[...] = jnp.sum(sland[...], axis=0)
    halo.wait()

    @pl.when(s != 31)
    def _():
        row = lax.broadcasted_iota(jnp.int32, (64, 128), 0)
        end = slice(NATURAL, NATURAL + 64)
        ext[end, :] = jnp.where(row >= 64 - 2 * (s + 1), hal[...], ext[end, :])

    @pl.when(s == 31)
    def _():
        def gather(i, total):
            remote(nrm_ref, nland.at[i], ms.at[0], mr.at[i], core).wait_recv()
            return total + nland[i]

        total = lax.fori_loop(0, 31, gather, nrm_ref[...])
        for k in range(8):
            ext[pl.ds(base + 8 * 384 + k, 8, stride=8), :] = total[:, 128 * k : 128 * k + 128]

    out_ref[...] = ext[64 : 64 + NATURAL, :]
    for copy in far + opposite + beside + [sibling] + near + across + later:
        copy.wait_send()

    @pl.when(z > 0)
    def _():
        for q in range(4):
            down(q).wait_send()

    def told(i, _):
        tell(i).wait_send()
        return 0

    lax.fori_loop(1, 32, told, 0)

    @pl.when(s != 31)
    def _():
        norm_send.wait_send()


def last_reduce(qkv_grads, normed_part, canonical, norm_part, squares):
    shape = jax.ShapeDtypeStruct
    unit = (3, 128, 256)
    room = pltpu.VMEM
    return pl.pallas_call(
        last_kernel,
        out_shape=(shape((NATURAL, 128), f32), shape((512, D), f32), shape((8, 128), f32)),
        in_specs=[VM] * 5,
        out_specs=(VM, VM, VM),
        scratch_shapes=[
            room((64 + NATURAL + 6, 128), f32), room((64, 128), f32), room((64, 128), f32),
            room((2,) + unit, bf), room((2,) + unit, bf), room(unit, bf), room((2,) + unit, bf),
            room((4,) + unit, bf), room((4,) + unit, bf), room((2,) + unit, bf),
            room((2, 2, 256, D), bf), room((2, 256, D), bf), room((2, 256, D), bf),
            room((32, 8, D), f32), room((32, 8, 128), f32),
            DMA((7,)), DMA((7,)), DMA((3, 2)), DMA((3, 2)), DMA((4,)), DMA((4,)),
            DMA((1,)), DMA((32,)), DMA((32,)), DMA((32,)), DMA((2,)),
        ],
        compiler_params=params_for(3),
    )(qkv_grads, normed_part, canonical, norm_part, squares)


def swap_kernel(n, to_tokens, a_ref, o_ref, ss, rs, ls):
    me = lax.axis_index("fsdp")
    bar = pltpu.get_barrier_semaphore()
    for i in range(1, n):
        pl.semaphore_signal(
            bar, inc=1, device_id={"fsdp": lax.rem(me + i, n)}, device_id_type=MESH
        )
    pl.semaphore_wait(bar, n - 1)
    tokens = (a_ref if to_tokens else o_ref).shape[0] // n
    width = (o_ref if to_tokens else a_ref).shape[1] // n

    def token_block(ref, owner):
        return ref.at[pl.ds(pl.multiple_of(owner * tokens, 16), tokens)]

    def head_block(ref, owner):
        return ref.at[:, pl.ds(pl.multiple_of(owner * width, 128), width)]

    take, put = (token_block, head_block) if to_tokens else (head_block, token_block)
    local = pltpu.make_async_copy(take(a_ref, me), put(o_ref, me), ls)
    local.start()
    copies = []
    for i in range(1, n):
        to = lax.rem(me + i, n)
        copy = pltpu.make_async_remote_copy(
            src_ref=take(a_ref, to), dst_ref=put(o_ref, me), send_sem=ss.at[i], recv_sem=rs.at[i],
            device_id={"fsdp": to}, device_id_type=MESH,
        )
        copy.start()
        copies.append(copy)
    for i in range(1, n):
        copies[i - 1].wait_send()
        ref = put(o_ref, lax.rem(me - i + n, n))
        pltpu.make_async_remote_copy(
            src_ref=ref, dst_ref=ref, send_sem=ss.at[i], recv_sem=rs.at[i],
            device_id={"fsdp": lax.rem(me + i, n)}, device_id_type=MESH,
        ).wait_recv()
    local.wait()


def swap(array, n, to_tokens, collective):
    rows, columns = array.shape
    shape = (rows // n, columns * n) if to_tokens else (rows * n, columns // n)
    return pl.pallas_call(
        functools.partial(swap_kernel, n, to_tokens),
        out_shape=jax.ShapeDtypeStruct(shape, bf),
        in_specs=[VM],
        out_specs=VM,
        scratch_shapes=[DMA((n,)), DMA((n,)), DMA],
        compiler_params=params_for(collective, 32),
    )(array)


def partner(values):
    width = values.shape[-1]
    lane = lax.broadcasted_iota(jnp.int32, values.shape, values.ndim - 1)
    after = pltpu.roll(values, width - 32, values.ndim - 1)
    before = pltpu.roll(values, 32, values.ndim - 1)
    return jnp.where(lane % 64 < 32, after, before)


def qkv_kernel(h_ref, n_ref, w_ref, c_ref, s_ref, o_ref, q_ref, k_ref, v_ref):
    rows = h_ref[...].astype(f32)
    center = rows - jnp.mean(rows, axis=-1, keepdims=True)
    inverse = lax.rsqrt(jnp.mean(center * center, axis=-1, keepdims=True) + EPSILON)
    normed = (center * inverse * n_ref[0:1, :] + n_ref[1:2, :]).astype(bf)
    o_ref[...] = normed
    for j, ref in enumerate((q_ref, k_ref, v_ref)):
        mixed = jnp.dot(normed, w_ref[j], preferred_element_type=f32)
        if j == 2:
            ref[...] = mixed.astype(bf)
        else:
            for at in range(0, mixed.shape[1], 128):
                part = mixed[:, at : at + 128]
                turned = part * c_ref[...] + partner(part) * s_ref[...]
                ref[:, at : at + 128] = turned.astype(bf)


def project(hidden, norm_rows, w_qkv, cosine, sine):
    tokens, width = hidden.shape[0], w_qkv.shape[2]
    block = 256
    rows = lambda w: pl.BlockSpec((block, w), lambda i: (i, 0))
    full = lambda a: pl.BlockSpec(a.shape, lambda i: (0,) * a.ndim)
    shape = jax.ShapeDtypeStruct
    return pl.pallas_call(
        qkv_kernel,
        grid=(tokens // block,),
        in_specs=[rows(D), full(norm_rows), full(w_qkv), rows(128), rows(128)],
        out_specs=[rows(D), rows(width), rows(width), rows(width)],
        out_shape=[shape((tokens, D), bf)] + [shape((tokens, width), bf)] * 3,
        compiler_params=params_for(),
    )(hidden, norm_rows, w_qkv, cosine, sine)


NT = (((1,), (1,)), ((), ()))
TN = (((0,), (0,)), ((), ()))
BLOCK = 512


def one_head(pair, h):
    lane = lax.broadcasted_iota(jnp.int32, pair.shape, 1)
    return jnp.where((lane < 64) if h == 0 else (lane >= 64), pair, jnp.zeros_like(pair))


def causal(scores, i, j):
    key = j * scores.shape[0] + lax.broadcasted_iota(jnp.int32, scores.shape, 0)
    query = i * scores.shape[1] + lax.broadcasted_iota(jnp.int32, scores.shape, 1)
    return jnp.where(key <= query, scores, MASKED)


def attend_kernel(q_ref, k_ref, v_ref, o_ref, low_ref, l_ref):
    i = pl.program_id(1)
    heads = [one_head(q_ref[...], h) for h in range(2)]

    def block(j, carry, masked):
        at = pl.ds(pl.multiple_of(j * BLOCK, BLOCK), BLOCK)
        keys, values = k_ref[at, :], v_ref[at, :]
        out = []
        for h in range(2):
            peak, total, summed = carry[3 * h : 3 * h + 3]
            scores = lax.dot_general(keys, heads[h], NT, preferred_element_type=f32)
            scores = scores * (SCALE * LOG2E)
            if masked:
                scores = causal(scores, i, j)
            new_peak = jnp.maximum(peak, jnp.max(scores, axis=0, keepdims=True))
            weights = jnp.exp2(scores - new_peak)
            shrink = jnp.exp2(peak - new_peak)
            total = total * shrink + jnp.sum(weights, axis=0, keepdims=True)
            part = lax.dot_general(
                values[:, 64 * h : 64 * h + 64], weights.astype(bf), TN, preferred_element_type=f32
            )
            out += [new_peak, total, summed * shrink + part]
        return tuple(out)

    start = (
        jnp.full((1, BLOCK), MASKED, f32), jnp.zeros((1, BLOCK), f32), jnp.zeros((64, BLOCK), f32)
    ) * 2
    carry = lax.fori_loop(0, i, lambda j, carry: block(j, carry, False), start)
    peak0, total0, sum0, peak1, total1, sum1 = block(i, carry, True)
    out = jnp.concatenate([sum0 / total0, sum1 / total1], axis=0).T
    o_ref[...] = out
    low_ref[...] = out.astype(bf)
    logs = jnp.concatenate([peak0 + jnp.log2(total0), peak1 + jnp.log2(total1)], axis=0)
    l_ref[...] = logs.reshape(1, 2, BLOCK)


def attend(queries, keys, values):
    tokens, width = queries.shape
    pairs = width // 128
    block = pl.BlockSpec((BLOCK, 128), lambda p, i: (i, p))
    full = pl.BlockSpec((tokens, 128), lambda p, i: (0, p))
    logs = pl.BlockSpec((1, 2, BLOCK), lambda p, i: (p, 0, i))
    shape = jax.ShapeDtypeStruct
    return pl.pallas_call(
        attend_kernel,
        grid=(pairs, tokens // BLOCK),
        in_specs=[block, full, full],
        out_specs=[block, block, logs],
        out_shape=[
            shape((tokens, width), f32), shape((tokens, width), bf), shape((pairs, 2, tokens), f32)
        ],
        compiler_params=params_for(),
    )(queries, keys, values)


def attend_back_kernel(
    q_ref, k_ref, v_ref, g_ref, a_ref, l_ref, cq_ref, sq_ref, c_ref, s_ref,
    dq_ref, dk_ref, dv_ref, dk, dv,
):
    i = pl.program_id(1)

    @pl.when(i == 0)
    def _():
        dk[...] = jnp.zeros_like(dk)
        dv[...] = jnp.zeros_like(dv)

    queries, grads = q_ref[...], g_ref[...]
    heads = [one_head(queries, h) for h in range(2)]
    grad_heads = [one_head(grads, h) for h in range(2)]
    both_heads = jnp.concatenate(heads, axis=0)
    both_grads = jnp.concatenate(grad_heads, axis=0)
    products = (a_ref[...] * grads.astype(f32)).T
    dots = [jnp.sum(products[64 * h : 64 * h + 64], axis=0, keepdims=True) for h in range(2)]
    logs = l_ref[0]

    def block(j, sums, masked):
        at = pl.ds(pl.multiple_of(j * BLOCK, BLOCK), BLOCK)
        keys, values = k_ref[at, :], v_ref[at, :]
        weights, score_grads = [], []
        for h in range(2):
            scores = lax.dot_general(keys, heads[h], NT, preferred_element_type=f32)
            scores = scores * (SCALE * LOG2E)
            if masked:
                scores = causal(scores, i, j)
            prob = jnp.exp2(scores - logs[h : h + 1])
            prob_grad = lax.dot_general(values, grad_heads[h], NT, preferred_element_type=f32)
            score_grads.append((prob * (prob_grad - dots[h])).astype(bf))
            weights.append(prob.astype(bf))
        dv[at, :] += jnp.dot(
            jnp.concatenate(weights, axis=1), both_grads, preferred_element_type=f32
        )
        dk[at, :] += jnp.dot(
            jnp.concatenate(score_grads, axis=1), both_heads, preferred_element_type=f32
        )
        return tuple(
            sums[h] + lax.dot_general(score_grads[h], keys, TN, preferred_element_type=f32)
            for h in range(2)
        )

    zero = jnp.zeros((BLOCK, 128), f32)
    sums = lax.fori_loop(0, i, lambda j, sums: block(j, sums, False), (zero, zero))
    sums = block(i, sums, True)
    lane = lax.broadcasted_iota(jnp.int32, zero.shape, 1)
    query_grad = jnp.where(lane < 64, sums[0], sums[1]) * SCALE
    dq_ref[...] = (query_grad * cq_ref[...] - partner(query_grad) * sq_ref[...]).astype(bf)

    @pl.when(i == pl.num_programs(1) - 1)
    def _():
        def turn(t, _):
            at = pl.ds(pl.multiple_of(t * 256, 256), 256)
            key_grad = dk[at, :] * SCALE
            turned = key_grad * c_ref[at, :] - partner(key_grad) * s_ref[at, :]
            dk_ref[at, :] = turned.astype(bf)
            dv_ref[at, :] = dv[at, :].astype(bf)
            return 0

        lax.fori_loop(0, dk.shape[0] // 256, turn, 0)


def attend_back(queries, keys, values, grads, attended, logs, cosine, sine):
    tokens, width = queries.shape
    block = pl.BlockSpec((BLOCK, 128), lambda p, i: (i, p))
    full = pl.BlockSpec((tokens, 128), lambda p, i: (0, p))
    table_block = pl.BlockSpec((BLOCK, 128), lambda p, i: (i, 0))
    table = pl.BlockSpec((tokens, 128), lambda p, i: (0, 0))
    log_block = pl.BlockSpec((1, 2, BLOCK), lambda p, i: (p, 0, i))
    return pl.pallas_call(
        attend_back_kernel,
        grid=(width // 128, tokens // BLOCK),
        in_specs=[block, full, full, block, block, log_block, table_block, table_block, table, table],
        out_specs=[block, full, full],
        out_shape=[jax.ShapeDtypeStruct((tokens, width), bf)] * 3,
        scratch_shapes=[pltpu.VMEM((tokens, 128), f32), pltpu.VMEM((tokens, 128), f32)],
        compiler_params=params_for(),
    )(queries, keys, values, grads, attended, logs, cosine, sine, cosine, sine)


def norm_forward(values, gain_row, shift_row):
    center = values - jnp.mean(values, axis=-1, keepdims=True)
    spread = jnp.mean(center * center, axis=-1, keepdims=True)
    inverse = lax.rsqrt(spread + EPSILON)
    unit_rows = center * inverse
    return (unit_rows * gain_row + shift_row, unit_rows, inverse)


def norm_backward(grad_rows, unit_rows, inverse, gain_row):
    scaled = grad_rows * gain_row
    first_mean = jnp.mean(scaled, axis=-1, keepdims=True)
    second_mean = jnp.mean(scaled * unit_rows, axis=-1, keepdims=True)
    return inverse * (scaled - first_mean - unit_rows * second_mean)


def norm_sums(grad_rows, unit_rows):
    return jnp.sum(grad_rows * unit_rows, axis=0), jnp.sum(grad_rows, axis=0)


def up_from_shards(rows):
    pieces = [rows[:128].reshape(1, 4, 32, D), rows[128:3968].reshape(10, 4, 96, D)]
    pieces.append(rows[3968:].reshape(1, 4, 32, D))
    return jnp.concatenate(
        [piece.transpose(0, 2, 1, 3).reshape(-1, FF) for piece in pieces], axis=0
    )


def up_to_shards(grad):
    pieces = [(grad[:32], 1, 32), (grad[32:992], 10, 96), (grad[992:], 1, 32)]
    return jnp.concatenate(
        [
            piece.reshape(blocks, rows, 4, D).transpose(0, 2, 1, 3).reshape(-1, D)
            for piece, blocks, rows in pieces
        ],
        axis=0,
    )


def dots(a, b, contract):
    return lax.dot_general(a, b, ((contract[:1], contract[1:]), ((), ())), preferred_element_type=f32)


def per_device(lines, hidden_in, params, cotangent, source_ids, corpus_weight, positions):
    devices = lax.axis_size(("dp", "fsdp"))
    width = lax.axis_size("fsdp")
    hidden = hidden_in[0]
    tokens = hidden.shape[0]
    place = lax.axis_index("fsdp")
    if lines:
        places = jnp.pad(positions.astype(f32).reshape(4, 128), ((0, 4), (0, 0)))
        hidden_all, w_qkv, canonical, norm_rows, places = first_gather(
            params.reshape(NATURAL, 128), hidden, places
        )
        places = places[:, :4].reshape(-1)
    else:
        whole = lax.all_gather(params, ("dp", "fsdp"), axis=0, tiled=True)
        ends = [0, 3 * D * D, 4 * D * D, 4 * D * D + D * FF, 4 * D * D + 2 * D * FF]
        parts = [whole[a:b] for a, b in zip(ends, ends[1:])]
        w_qkv = lax.dynamic_index_in_dim(
            parts[0].reshape(D, 3, width, D // width).transpose(1, 2, 0, 3), place, 1, False
        )
        w_out, w_up, w_down = parts[1].reshape(D, D), parts[2].reshape(D, FF), parts[3].reshape(FF, D)
        norm_rows = whole[ends[-1] :].reshape(8, D).astype(f32)
        hidden_all = lax.all_gather(hidden, "fsdp", axis=0, tiled=True)
        places = lax.all_gather(positions[0].astype(f32), "fsdp", axis=0, tiled=True)

    lane = jnp.arange(128) % 64
    frequency = jnp.exp((lane % 32).astype(f32) * (-2.0 * math.log(10000.0) / HEAD_DIM))
    angles = places[:, None] * frequency
    cosine = jnp.cos(angles)
    sine = jnp.where(lane < 32, -1.0, 1.0) * jnp.sin(angles)
    normed_all, queries, keys, values = project(hidden_all, norm_rows, w_qkv, cosine, sine)
    attended_all, attended_low, logs = attend(queries, keys, values)
    attended = swap(attended_low, width, True, 4)
    if lines:
        others = gather_others(canonical)
        w_out, w_up, w_down = others[:D], up_from_shards(others[D : 5 * D]), others[5 * D :]

    inputs = hidden.astype(f32)
    branch = dots(attended, w_out, (1, 0))
    branch_norm, branch_unit, branch_inverse = norm_forward(branch, norm_rows[2], norm_rows[3])
    residual = inputs + branch_norm
    entered, entered_unit, entered_inverse = norm_forward(residual, norm_rows[4], norm_rows[5])
    entered_low = entered.astype(bf)
    lifted = dots(entered_low, w_up, (1, 0))
    activated = jax.nn.gelu(lifted).astype(bf)
    lowered = dots(activated, w_down, (1, 0))
    lowered_norm, lowered_unit, lowered_inverse = norm_forward(lowered, norm_rows[6], norm_rows[7])
    output = (residual + lowered_norm).astype(bf)
    squares = jnp.stack([jnp.mean(branch * branch), jnp.mean(lowered * lowered)])

    source_table = jnp.arange(corpus_weight.shape[0], dtype=jnp.int32)
    row_scale = jnp.sum(jnp.where(source_ids[0] == source_table, corpus_weight, 0.0))
    upstream = cotangent[0].astype(f32) * row_scale
    lowered_grad = norm_backward(upstream, lowered_unit, lowered_inverse, norm_rows[6]).astype(bf)
    grad_down = dots(activated, lowered_grad, (0, 0))
    activated_grad = dots(lowered_grad, w_down, (1, 1))
    lifted_grad = jax.vjp(jax.nn.gelu, lifted)[1](activated_grad)[0].astype(bf)
    grad_up = dots(entered_low, lifted_grad, (0, 0))
    entered_grad = dots(lifted_grad, w_up, (1, 1))
    residual_grad = upstream + norm_backward(
        entered_grad, entered_unit, entered_inverse, norm_rows[4]
    )
    branch_grad = norm_backward(residual_grad, branch_unit, branch_inverse, norm_rows[2]).astype(bf)
    grad_out = dots(attended, branch_grad, (0, 0))
    attended_grad = dots(branch_grad, w_out, (1, 1)).astype(bf)
    if lines:
        flat = jnp.concatenate(
            [grad_out.astype(bf), up_to_shards(grad_up.astype(bf)), grad_down.astype(bf)], axis=0
        )
        owned = reduce_others(flat)

    grads_all = swap(attended_grad, width, False, 5)
    mixed_grad = attend_back(
        queries, keys, values, grads_all, attended_all, logs, cosine, sine
    )
    grad_qkv = jnp.stack([dots(normed_all, part, (0, 0)) for part in mixed_grad])
    normed_part = sum(dots(part, w_qkv[j], (1, 1)) for j, part in enumerate(mixed_grad))
    _, unit_all, _ = norm_forward(hidden_all.astype(f32), norm_rows[0], norm_rows[1])
    norm_part = jnp.stack(
        [
            *norm_sums(normed_part, unit_all),
            *norm_sums(residual_grad, branch_unit),
            *norm_sums(entered_grad, entered_unit),
            *norm_sums(upstream, lowered_unit),
        ]
    )
    if lines:
        told = jnp.zeros((8, 128), f32).at[0, :2].set(squares)
        param_grads, normed_grad, told = last_reduce(
            grad_qkv.astype(bf), normed_part.astype(bf), owned, norm_part, told
        )
        param_grads = param_grads.reshape(-1)
        squares = told[0, :2]
    else:
        spread = jnp.zeros((3, width, D, D // width), f32)
        spread = lax.dynamic_update_slice_in_dim(spread, grad_qkv[:, None], place, 1)
        flat = jnp.concatenate(
            [
                part.reshape(-1)
                for part in (spread.transpose(2, 0, 1, 3), grad_out, grad_up, grad_down, norm_part)
            ]
        )
        param_grads = lax.psum_scatter(flat, ("dp", "fsdp"), scatter_dimension=0, tiled=True)
        normed_grad = lax.psum_scatter(normed_part, "fsdp", scatter_dimension=0, tiled=True)
        squares = lax.psum(squares, ("dp", "fsdp"))
    statistics = squares / devices
    _, normed_unit, normed_inverse = norm_forward(inputs, norm_rows[0], norm_rows[1])
    into_input = norm_backward(normed_grad, normed_unit, normed_inverse, norm_rows[0])
    input_grad = (residual_grad + into_input).astype(bf)
    return (output[None], input_grad[None], param_grads, statistics)


def solution(mesh):
    lines = (mesh.shape["dp"], mesh.shape["fsdp"]) == (8, 4)
    in_specs = (
        P("dp", "fsdp", None),
        P(("dp", "fsdp")),
        P("dp", "fsdp", None),
        P("dp"),
        P(),
        P("dp", "fsdp"),
    )
    out_specs = (P("dp", "fsdp", None), P("dp", "fsdp", None), P(("dp", "fsdp")), P())
    return jax.shard_map(
        functools.partial(per_device, lines),
        mesh=mesh,
        in_specs=in_specs,
        out_specs=out_specs,
        check_vma=False,
    )
```

time: 1920 us -> 602 us (0.31)
  waiting for transfers between devices: 997 us -> 0 us
  Pallas kernels: 0 us -> 393 us
  matrix products: 382 us -> 79.9 us
  other arithmetic: 217 us -> 26.7 us
  local copies, waits for them, and re-layouts: 255 us -> 92.9 us
  blocking collectives: 42.2 us -> 0 us
    unnamed x7 -> x0, waiting for transfers between devices: 676 us -> none
    pallas_call x0 -> x9, Pallas kernels: none -> 393 us  [the longest x1 91 us: gather_others(): pl.pallas_call(gather_kernel, out_shape=jax.ShapeDtypeStruct((24 * SHARD,...]
    dot_general x156 -> x15, matrix products: 382 us -> 79.9 us  [dots(): lax.dot_general(a, b, ((contract[:1], contract[1:]), ((), ())), preferred...]
    all_gather x3 -> x0, waiting for transfers between devices: 283 us -> none  [the longest x1 277 us: fetch_forward(): whole = lax.all_gather(shard_part, ('dp', 'fsdp'), axis=0, tiled=True)]
    all_gather x1 -> x0, other arithmetic: 149 us -> none  [fetch_forward(): whole = lax.all_gather(shard_part, ('dp', 'fsdp'), axis=0, tiled=True)]
    unnamed x224 -> x69, local copies, waits for them, and re-layouts: 149 us -> 43.8 us
    slice x23 -> x6, local copies, waits for them, and re-layouts: 78.3 us -> 14.8 us  [the longest x2 7.43 us: up_to_shards(): pieces = [(grad[:32], 1, 32), (grad[32:992], 10, 96), (grad[992:], 1, 32)]]
    psum x1 -> x0, blocking collectives: 42.2 us -> none  [per_device(): lax.psum(local_squares, ('dp', 'fsdp')) / lax.axis_size(('dp', 'fsdp'))]
  transfers between devices with their start and end apart: 6 -> 0, of which waited for: 4 -> 0; matrix products, arithmetic and copies ran while one was open for 6% -> 0% of each run, Pallas kernels for 0% -> 0%
where the time goes in v1:
time: 602 us; the launch traced here: 596 us
  Pallas kernels  393 us (65%)
  local copies, waits for them, and re-layouts  92.9 us (15%)
  matrix products  79.9 us (13%)
  other arithmetic  26.7 us (4%)
    pallas_call x1, Pallas kernels, gather_others(): pl.pallas_call(gather_kernel, out_shape=jax.ShapeDtypeStruct((24 * SHARD,...  91 us
    pallas_call x1, Pallas kernels, reduce_others(): pl.pallas_call(reduce_kernel, out_shape=jax.ShapeDtypeStruct((SHARD, D),...  85.5 us
    dot_general x15, matrix products, dots(): lax.dot_general(a, b, ((contract[:1], contract[1:]), ((), ())), preferred...  79.9 us
    pallas_call x1, Pallas kernels, last_reduce(): pl.pallas_call(last_kernel, out_shape=(shape((NATURAL, 128), f32), shape(...  68.2 us
    unnamed x69, local copies, waits for them, and re-layouts  43.8 us
    pallas_call x1, Pallas kernels, first_gather(): pl.pallas_call(first_kernel, out_shape=(shape((2048, D), bf), shape((3, D...  42 us
    pallas_call x1, Pallas kernels, attend_back(): pl.pallas_call(attend_back_kernel, grid=(width // 128, tokens // BLOCK),...  41.1 us
    pallas_call x2, Pallas kernels, swap(): pl.pallas_call(functools.partial(swap_kernel, n, to_tokens), out_shape=ja...  27.9 us

profile of v1, /device:TPU:5, one launch (start us, length us, event | category | flops | bytes accessed | tf_op | source)
XLA Modules:
  0.0 596.5 jit_solution(15404983350279884998)
XLA Ops:
  0.6 0.7 convert_element_type.60
  1.3 1.2 copy-done.3
  2.6 1.1 copy-done.12
  3.7 42.0 %shard_map.93 = (bf16[2048,1024]{1,0:T(8,128)(2,1)S(1)}, bf16[3,1024,256]{2,1,0:T(8,128)(2,1)S(1)}, bf16[384,1024]{1,0:T(8,128)(2,1)S(1)}, f32[8,1024]{1,0:T(8,128)S(1)}, f32[4,8,128]{2,1,0:T(8,128)S(1)}) custom-call(bf16[3074,128]{1,0:T(8,128)(2,1)S(1)} %bitcast.113, bf16[512,1024]{1,0:T(8,128)(2,1)S(1)} %bitcast.111, f32[8,128]{1,0:T(8,128)S(1)} %pad.9.pos_ref), custom_call_target="tpu_custom_call" | custom-call | tf_op jit(solution)/shard_map/pallas_call | solution.py:287
  45.7 2.1 copy-done
  47.8 91.0 %shard_map.97 = bf16[9216,1024]{1,0:T(8,128)(2,1)S(1)} custom-call(bf16[384,1024]{1,0:T(8,128)(2,1)S(1)} %get-tuple-element.42.c_ref), custom_call_target="tpu_custom_call" | custom-call | tf_op jit(solution)/shard_map/pallas_call | solution.py:451
  138.8 6.5 %copy-done.2 = bf16[9216,1024]{1,0:T(8,128)(2,1)} copy-done((bf16[9216,1024]{1,0:T(8,128)(2,1)}, bf16[9216,1024]{1,0:T(8,128)(2,1)S(1)}, u32[]{:S(2)}) %copy-start.2) | copy-done | bytes 18874392
  145.6 0.7 constant_dynamic-update-slice_fusion.2
  146.3 7.3 %slice.90 = bf16[3840,1024]{1,0:T(8,128)(2,1)} slice(bf16[9216,1024]{1,0:T(8,128)(2,1)} %copy-done.2), slice={[1152:4992], [0:1024]} | slice | bytes 15728640 | tf_op jit(solution)/shard_map/slice | solution.py:1159
  153.7 12.5 %copy.14 = bf16[10,4,96,1024]{3,1,2,0:T(4,128)(2,1)} copy(bf16[10,4,96,1024]{3,2,1,0:T(8,128)(2,1)} %bitcast.117) | data formatting | bytes 15728640 | tf_op jit(solution)/shard_map/reshape | solution.py:1159
  166.1 8.6 %copy.20 = bf16[120,8,4,1024]{3,1,2,0:T(8,128)(2,1)S(1)} copy(bf16[120,8,4,1024]{3,2,1,0:T(4,128)(2,1)} %bitcast.116) | data formatting | bytes 15728640
  174.7 4.0 constant_dynamic-update-slice_fusion.1
  179.0 0.7 constant_dynamic-update-slice_fusion
  179.8 3.7 fusion.41
  183.6 11.6 %shard_map.94 = (bf16[2048,1024]{1,0:T(8,128)(2,1)}, bf16[2048,256]{1,0:T(8,128)(2,1)S(1)}, bf16[2048,256]{1,0:T(8,128)(2,1)S(1)}, bf16[2048,256]{1,0:T(8,128)(2,1)S(1)}) custom-call(bf16[2048,1024]{1,0:T(8,128)(2,1)} %copy-done, f32[8,1024]{1,0:T(8,128)S(1)} %get-tuple-element.35.n_ref, bf16[3,1024,256]{2,1,0:T(8,128)(2,1)} %copy-done.8, ...), custom_call_target="tpu_custom_call" | custom-call | tf_op jit(solution)/shard_map/pallas_call | solution.py:976
  195.2 26.1 %shard_map.95 = (f32[2048,256]{1,0:T(8,128)}, bf16[2048,256]{1,0:T(8,128)(2,1)S(1)}, f32[2,2,2048]{2,1,0:T(2,128)S(1)}) custom-call(bf16[2048,256]{1,0:T(8,128)(2,1)S(1)} %get-tuple-element.38.q_ref, bf16[2048,256]{1,0:T(8,128)(2,1)S(1)} %get-tuple-element.39.k_ref, bf16[2048,256]{1,0:T(8,128)(2,1)S(1)} %get-tuple-element.40.v_ref), custom_call_target="tpu_custom_call" | custom-call | tf_op jit(solution)/shard_map/pallas_call | solution.py:1045
  221.3 14.0 %shard_map.96 = bf16[512,1024]{1,0:T(8,128)(2,1)S(1)} custom-call(bf16[2048,256]{1,0:T(8,128)(2,1)S(1)} %get-tuple-element.41.a_ref), custom_call_target="tpu_custom_call" | custom-call | tf_op jit(solution)/shard_map/pallas_call | solution.py:935
  235.3 3.1 fusion.63
  238.8 0.8 copy-done.4
  239.8 1.1 fusion.59
  241.4 4.7 fusion.57
  246.1 3.4 copy-done.25
  249.4 8.7 %fusion.64 = (f32[512]{0:T(512)S(1)}, f32[512,1024]{1,0:T(8,128)S(1)}) fusion(bf16[9216,1024]{1,0:T(8,128)(2,1)} %copy-done.2, f32[512,4096]{1,0:T(8,128)S(1)} %fusion.57), kind=kOutput, calls=%fused_computation.134 | convolution fusion | flops 4314365440 | bytes 18876416 | tf_op jit(solution)/shard_map/dot_general | solution.py:1178
  258.9 0.7 fusion.55
  259.6 0.3 multiply_reduce_fusion.7
  260.1 4.1 fusion.26
  264.2 14.0 %fusion.11 = bf16[512,4096]{1,0:T(8,128)(2,1)S(1)} fusion(f32[512,4096]{1,0:T(8,128)} %copy-done.25, bf16[9216,1024]{1,0:T(8,128)(2,1)} %copy-done.2, bf16[1,512,1024]{2,1,0:T(8,128)(2,1)S(1)} %copy-done.17, f32[512,1024]{1,0:T(8,128)S(1)} %get-tuple-element.91, f32[512]{0:T(512)S(1)} %broadcast_multiply_fusion.8, f32[512]{0:T(512)S(1)} %broadcast_multiply_fusion.9, ...), kind=kOutput, calls=%fused_computation.15 | convolution fusion | flops 4342153216 | bytes 24130048 | tf_op jit(solution)/shard_map/dot_general | solution.py:1178
  278.2 9.0 %multiply_reduce_fusion.2 = (f32[1024]{0:T(1024)S(1)}, f32[512]{0:T(512)S(1)}, f32[512]{0:T(512)S(1)}, f32[1024]{0:T(1024)S(1)}, f32[512,1024]{1,0:T(8,128)S(1)}) fusion(f32[512,1024]{1,0:T(8,128)S(1)} %get-tuple-element.71, f32[512]{0:T(512)S(1)} %add_rsqrt_fusion.3, f32[512]{0:T(512)S(1)} %broadcast_multiply_fusion.11, f32[1024]{0:T(1024)S(1)} %bitcast.133, ...), kind=kOutput, calls=%fused_computation.43 | convolution fusion | flops 4299682816 | bytes 16797696 | tf_op jit(solution)/shard_map/dot_general | solution.py:1178
  287.3 3.8 multiply_reduce_fusion.3
  291.1 0.6 multiply_convert_fusion.1
  291.8 0.6 copy-done.15
  292.4 1.0 copy-done.21
  293.4 2.9 fusion.33.a_ref
  296.3 13.8 %shard_map.98.g_ref = bf16[2048,256]{1,0:T(8,128)(2,1)S(1)} custom-call(bf16[512,1024]{1,0:T(8,128)(2,1)S(1)} %fusion.33.a_ref), custom_call_target="tpu_custom_call" | custom-call | tf_op jit(solution)/shard_map/pallas_call | solution.py:935
  310.2 1.0 copy-done.11
  311.1 41.1 %shard_map.99 = (bf16[2048,256]{1,0:T(8,128)(2,1)S(1)}, bf16[2048,256]{1,0:T(8,128)(2,1)S(1)}, bf16[2048,256]{1,0:T(8,128)(2,1)S(1)}) custom-call(bf16[2048,256]{1,0:T(8,128)(2,1)S(1)} %get-tuple-element.38.q_ref, bf16[2048,256]{1,0:T(8,128)(2,1)S(1)} %get-tuple-element.39.k_ref, bf16[2048,256]{1,0:T(8,128)(2,1)} %copy-done.10, ...), custom_call_target="tpu_custom_call" | custom-call | tf_op jit(solution)/shard_map/pallas_call | solution.py:1128
  352.2 1.3 fusion.38
  353.5 1.3 fusion.37
  354.9 1.3 fusion.36
  356.2 1.3 pad_maximum_fusion.v_ref
  357.5 0.6 convert_reduce_fusion
  358.1 1.4 fusion.2
  359.6 1.3 fusion.47
  360.9 4.5 fusion.45
  365.4 6.8 %fusion.58 = (f32[1024]{0:T(1024)S(1)}, f32[1024]{0:T(1024)S(1)}, bf16[2048,1024]{1,0:T(8,128)(2,1)}) fusion(f32[2048]{0:T(1024)S(1)} %add_rsqrt_fusion, f32[2048]{0:T(1024)S(1)} %broadcast_multiply_fusion, bf16[2048,1024]{1,0:T(8,128)(2,1)S(1)} %copy-done.1, bf16[2048,256]{1,0:T(8,128)(2,1)S(1)} %get-tuple-element.48, ...), kind=kOutput, calls=%fused_computation.128 | convolution fusion | flops 1092614144 | bytes 26763264 | tf_op jit(solution)/shard_map/dot_general | solution.py:1178
  372.2 2.6 convert_dynamic-update-slice_fusion.1
  374.8 0.9 copy-done.27
  375.8 5.3 convolution_convert_fusion
  381.1 3.3 copy-done.20
  384.6 0.7 constant_dynamic-update-slice_fusion.5
  385.4 7.4 %slice.104 = bf16[960,4096]{1,0:T(8,128)(2,1)} slice(bf16[1024,4096]{1,0:T(8,128)(2,1)} %copy-done.20), slice={[32:992], [0:4096]} | slice | bytes 15728640 | tf_op jit(solution)/shard_map/slice | solution.py:1167
  392.8 13.8 %reshape.218 = bf16[10,96,4,1024]{3,2,1,0:T(4,128)(2,1)} reshape(bf16[960,4096]{1,0:T(8,128)(2,1)} %slice.104) | data formatting | bytes 15728640 | tf_op jit(solution)/shard_map/reshape | solution.py:1170
  406.6 6.3 %copy.17 = bf16[10,96,4,1024]{3,1,2,0:T(8,128)(2,1)S(1)} copy(bf16[10,96,4,1024]{3,2,1,0:T(4,128)(2,1)} %reshape.218) | data formatting | bytes 15728640 | tf_op jit(solution)/shard_map/reshape | solution.py:1170
  412.9 4.1 constant_dynamic-update-slice_fusion.4
  417.2 0.7 constant_dynamic-update-slice_fusion.3
  418.0 13.0 %convert_dynamic-update-slice_fusion.g_ref = bf16[9216,1024]{1,0:T(8,128)(2,1)} fusion(bf16[9216,1024]{1,0:T(8,128)(2,1)} %constant_dynamic-update-slice_fusion.3, f32[512,4096]{1,0:T(8,128)} %copy-done.25, bf16[1,512,1024]{2,1,0:T(8,128)(2,1)} %param.10, f32[512,1024]{1,0:T(8,128)} %copy-done.19, f32[512]{0:T(512)S(1)} %broadcast_multiply_fusion.8, ...), kind=kOutput, calls=%fused_computation.16 | convolution fusion | flops 4323278848 | bytes 19935744 | tf_op jit(solution)/shard_map/dot_general | solution.py:1178
  431.0 85.5 %shard_map.100.can_ref = f32[384,1024]{1,0:T(8,128)S(1)} custom-call(bf16[9216,1024]{1,0:T(8,128)(2,1)} %convert_dynamic-update-slice_fusion.g_ref), custom_call_target="tpu_custom_call" | custom-call | tf_op jit(solution)/shard_map/pallas_call | solution.py:646
  516.5 0.9 fusion.27
  518.8 1.4 copy-done.7
  520.2 68.2 %shard_map.101 = (f32[3074,128]{1,0:T(8,128)S(1)}, f32[512,1024]{1,0:T(8,128)}, f32[8,128]{1,0:T(8,128)S(1)}) custom-call(bf16[3,1024,256]{2,1,0:T(8,128)(2,1)S(1)} %copy-done.7, bf16[2048,1024]{1,0:T(8,128)(2,1)} %get-tuple-element.74.n_ref, f32[384,1024]{1,0:T(8,128)S(1)} %shard_map.100.can_ref, f32[8,1024]{1,0:T(8,128)S(1)} %stack.64.nrm_ref, ...), custom_call_target="tpu_custom_call" | custom-call | tf_op jit(solution)/shard_map/pallas_call | solution.py:875
  588.4 2.5 multiply_reduce_fusion.10
  590.9 3.3 fusion.43
  594.3 0.5 multiply_bitcast_fusion
  594.8 1.2 copy.30
  (87 shorter events, 2.6 us)
Async XLA Ops:
  1.3 1.2 copy-start.3
  2.5 1.1 copy-start.12
  45.7 2.1 copy-start
  47.8 91.0 %copy-start.8 = (bf16[3,1024,256]{2,1,0:T(8,128)(2,1)}, bf16[3,1024,256]{2,1,0:T(8,128)(2,1)S(1)}, u32[]{:S(2)}) copy-start(bf16[3,1024,256]{2,1,0:T(8,128)(2,1)S(1)} %get-tuple-element.36.w_ref) | copy-start | bytes 4718596
  138.8 6.5 %copy-start.2 = (bf16[9216,1024]{1,0:T(8,128)(2,1)}, bf16[9216,1024]{1,0:T(8,128)(2,1)S(1)}, u32[]{:S(2)}) copy-start(bf16[9216,1024]{1,0:T(8,128)(2,1)S(1)} %shard_map.97) | copy-start | bytes 56623108
  183.5 11.6 %copy-start.5 = (f32[2048,128]{1,0:T(8,128)}, f32[2048,128]{1,0:T(8,128)S(1)}, u32[]{:S(2)}) copy-start(f32[2048,128]{1,0:T(8,128)S(1)} %get-tuple-element.86.s_ref.sq_ref) | copy-start | bytes 3145732
  183.5 11.6 %copy-start.6 = (f32[2048,128]{1,0:T(8,128)}, f32[2048,128]{1,0:T(8,128)S(1)}, u32[]{:S(2)}) copy-start(f32[2048,128]{1,0:T(8,128)S(1)} %get-tuple-element.87.c_ref.cq_ref) | copy-start | bytes 3145732
  195.2 40.1 %copy-start.10 = (bf16[2048,256]{1,0:T(8,128)(2,1)}, bf16[2048,256]{1,0:T(8,128)(2,1)S(1)}, u32[]{:S(2)}) copy-start(bf16[2048,256]{1,0:T(8,128)(2,1)S(1)} %get-tuple-element.40.v_ref) | copy-start | bytes 3145732
  235.3 6.0 %slice-start = ((s8[8388608]{0:T(1024)(128)(4,1)}), s8[4194304]{0:T(1024)(128)(4,1)S(1)}, s32[]{:S(2)}) async-start(s8[8388608]{0:T(1024)(128)(4,1)} %bitcast.147), calls=%async_computation | async-start | bytes 8388608
  238.4 1.2 copy-start.4
  238.4 3.0 slice-start.1
  241.0 46.3 %copy-start.13 = (f32[512,1024]{1,0:T(8,128)}, f32[512,1024]{1,0:T(8,128)S(1)}, u32[]{:S(2)}) copy-start(f32[512,1024]{1,0:T(8,128)S(1)} %get-tuple-element.71) | copy-start | bytes 6291460
  246.1 3.4 copy-start.25
  249.4 9.5 %copy-start.24 = (f32[16]{0:T(128)S(1)}, f32[16]{0:T(128)}, u32[]{:S(2)}) copy-start(f32[16]{0:T(128)} %param.12) | copy-start | bytes 196
  258.1 6.1 %copy-start.19 = (f32[512,1024]{1,0:T(8,128)}, f32[512,1024]{1,0:T(8,128)S(1)}, u32[]{:S(2)}) copy-start(f32[512,1024]{1,0:T(8,128)S(1)} %get-tuple-element.91) | copy-start | bytes 6291460
  258.1 2.0 copy-start.17
  278.2 9.1 %copy-start.26 = (bf16[512,4096]{1,0:T(8,128)(2,1)}, bf16[512,4096]{1,0:T(8,128)(2,1)S(1)}, u32[]{:S(2)}) copy-start(bf16[512,4096]{1,0:T(8,128)(2,1)S(1)} %fusion.11) | copy-start | bytes 12582916
  291.1 1.3 copy-start.15
  292.4 1.0 copy-start.21
  310.2 1.0 copy-start.11
  311.1 41.1 %copy-start.23 = (bf16[2048,1024]{1,0:T(8,128)(2,1)S(1)}, bf16[2048,1024]{1,0:T(8,128)(2,1)}, u32[]{:S(2)}) copy-start(bf16[2048,1024]{1,0:T(8,128)(2,1)} %get-tuple-element.43) | copy-start | bytes 12582916
  354.8 2.6 copy-start.1
  358.1 1.4 copy-start.9
  365.4 6.8 %copy-start.22 = (bf16[512,1024]{1,0:T(8,128)(2,1)S(1)}, bf16[512,1024]{1,0:T(8,128)(2,1)}, u32[]{:S(2)}) copy-start(bf16[512,1024]{1,0:T(8,128)(2,1)} %copy-done.21) | copy-start | bytes 3145732
  372.2 2.7 copy-start.14
  372.2 3.6 copy-start.27
  381.0 3.3 copy-start.20
  431.0 85.5 %copy-start.18 = (bf16[1,512,1024]{2,1,0:T(8,128)(2,1)S(1)}, bf16[1,512,1024]{2,1,0:T(8,128)(2,1)}, u32[]{:S(2)}) copy-start(bf16[1,512,1024]{2,1,0:T(8,128)(2,1)} %param.10) | copy-start | bytes 3145732
  518.8 1.4 copy-start.7
  588.4 2.5 copy-start.16

commit v2 on v1

--- a/solution.py
+++ b/solution.py
@@ -312,7 +312,7 @@
 OVER_X = 48
 
 
-def gather_kernel(c_ref, g_ref, ss, rs, ls):
+def gather_steps(c_ref, g_ref, ss, rs, ls, more):
     z, x, y, c = coords()
     xn, yn, cn = 1 - x, 1 - y, 1 - c
     to_x, to_y, to_core = dev(z, xn, y, c), dev(z, x, yn, c), dev(z, x, y, cn)
@@ -328,7 +328,7 @@
     def _():
         local.start()
 
-    meet_neighbours(z, x, y, c, [to_x, to_y, to_core])
+    meet_neighbours(z, x, y, c, [to_x, to_y, to_core] + more)
 
     @pl.when(z >= 1)
     def _():
@@ -425,8 +425,6 @@
 
         return 0
 
-    lax.fori_loop(0, UNITS + core_lag, step, 0)
-
     def finish(i, _):
         zz, _, _ = unit(i)
         for kind in (CO, CX, CY, CXD, CYD):
@@ -444,22 +442,11 @@
 
         return 0
 
-    lax.fori_loop(0, UNITS, finish, 0)
-
-
-def gather_others(canonical):
-    return pl.pallas_call(
-        gather_kernel,
-        out_shape=jax.ShapeDtypeStruct((24 * SHARD, D), bf),
-        in_specs=[VM],
-        out_specs=ANY,
-        scratch_shapes=[DMA((11, UNITS)), DMA((11, UNITS)), DMA],
-        compiler_params=params_for(1, 16),
-    )(canonical)
-
-
-def reduce_kernel(
-    g_ref, o_ref, lb, cb, xb, yb, dxb, dyb, zub, zdb, ss, rs, cs, cr, ls
+    return step, UNITS + core_lag, lambda: lax.fori_loop(0, UNITS, finish, 0)
+
+
+def reduce_steps(
+    g_ref, o_ref, lb, cb, xb, yb, dxb, dyb, zub, zdb, ss, rs, cs, cr, ls, more
 ):
     z, x, y, c = coords()
     xn, yn, cn = 1 - x, 1 - y, 1 - c
@@ -493,7 +480,7 @@
         return 0
 
     lax.fori_loop(0, UNITS, load_all, 0)
-    meet_neighbours(z, x, y, c, [to_x, to_y, to_core])
+    meet_neighbours(z, x, y, c, [to_x, to_y, to_core] + more)
 
     def send_all(i, _):
         for p in range(4):
@@ -617,8 +604,6 @@
 
         return 0
 
-    lax.fori_loop(0, UNITS + lag4, step, 0)
-
     def finish(i, _):
         zz, _ = unit(i)
         for p in range(4):
@@ -636,27 +621,20 @@
 
         return 0
 
-    lax.fori_loop(0, UNITS, finish, 0)
-
-
-def reduce_others(grads):
+    return step, UNITS + lag4, lambda: lax.fori_loop(0, UNITS, finish, 0)
+
+
+def reduce_rooms():
     def room(*shape):
         return pltpu.VMEM(shape + (D,), bf)
 
-    return pl.pallas_call(
-        reduce_kernel,
-        out_shape=jax.ShapeDtypeStruct((SHARD, D), f32),
-        in_specs=[ANY],
-        out_specs=VM,
-        scratch_shapes=[
-            room(UNITS, 4, CHUNK), room(UNITS, 4, CHUNK),
-            room(UNITS, CHUNK), room(UNITS, CHUNK),
-            room(UNITS, OVER_X), room(UNITS, CHUNK - OVER_X),
-            room(UNITS, CHUNK), room(UNITS, CHUNK),
-            DMA((6, UNITS)), DMA((6, UNITS)), DMA((UNITS, 4)), DMA((UNITS, 4)), DMA((UNITS, 4)),
-        ],
-        compiler_params=params_for(2),
-    )(grads)
+    return [
+        room(UNITS, 4, CHUNK), room(UNITS, 4, CHUNK),
+        room(UNITS, CHUNK), room(UNITS, CHUNK),
+        room(UNITS, OVER_X), room(UNITS, CHUNK - OVER_X),
+        room(UNITS, CHUNK), room(UNITS, CHUNK),
+        DMA((6, UNITS)), DMA((6, UNITS)), DMA((UNITS, 4)), DMA((UNITS, 4)), DMA((UNITS, 4)),
+    ]
 
 
 def last_kernel(
@@ -950,21 +928,22 @@
     return jnp.where(lane % 64 < 32, after, before)
 
 
-def qkv_kernel(h_ref, n_ref, w_ref, c_ref, s_ref, o_ref, q_ref, k_ref, v_ref):
-    rows = h_ref[...].astype(f32)
+def project_rows(rows, n_ref, w_ref, cosine, sine):
+    rows = rows.astype(f32)
     center = rows - jnp.mean(rows, axis=-1, keepdims=True)
     inverse = lax.rsqrt(jnp.mean(center * center, axis=-1, keepdims=True) + EPSILON)
     normed = (center * inverse * n_ref[0:1, :] + n_ref[1:2, :]).astype(bf)
-    o_ref[...] = normed
-    for j, ref in enumerate((q_ref, k_ref, v_ref)):
-        mixed = jnp.dot(normed, w_ref[j], preferred_element_type=f32)
-        if j == 2:
-            ref[...] = mixed.astype(bf)
-        else:
-            for at in range(0, mixed.shape[1], 128):
-                part = mixed[:, at : at + 128]
-                turned = part * c_ref[...] + partner(part) * s_ref[...]
-                ref[:, at : at + 128] = turned.astype(bf)
+    mixed = [jnp.dot(normed, w_ref[j], preferred_element_type=f32) for j in range(3)]
+    for j in range(2):
+        parts = [mixed[j][:, at : at + 128] for at in range(0, mixed[j].shape[1], 128)]
+        parts = [part * cosine + partner(part) * sine for part in parts]
+        mixed[j] = jnp.concatenate(parts, axis=1)
+    return [normed] + [part.astype(bf) for part in mixed]
+
+
+def qkv_kernel(h_ref, n_ref, w_ref, c_ref, s_ref, *out_refs):
+    for ref, part in zip(out_refs, project_rows(h_ref[...], n_ref, w_ref, c_ref[...], s_ref[...])):
+        ref[...] = part
 
 
 def project(hidden, norm_rows, w_qkv, cosine, sine):
@@ -999,9 +978,8 @@
     return jnp.where(key <= query, scores, MASKED)
 
 
-def attend_kernel(q_ref, k_ref, v_ref, o_ref, low_ref, l_ref):
-    i = pl.program_id(1)
-    heads = [one_head(q_ref[...], h) for h in range(2)]
+def attend_rows(i, queries, k_ref, v_ref):
+    heads = [one_head(queries, h) for h in range(2)]
 
     def block(j, carry, masked):
         at = pl.ds(pl.multiple_of(j * BLOCK, BLOCK), BLOCK)
@@ -1029,9 +1007,14 @@
     carry = lax.fori_loop(0, i, lambda j, carry: block(j, carry, False), start)
     peak0, total0, sum0, peak1, total1, sum1 = block(i, carry, True)
     out = jnp.concatenate([sum0 / total0, sum1 / total1], axis=0).T
+    logs = jnp.concatenate([peak0 + jnp.log2(total0), peak1 + jnp.log2(total1)], axis=0)
+    return out, logs
+
+
+def attend_kernel(q_ref, k_ref, v_ref, o_ref, low_ref, l_ref):
+    out, logs = attend_rows(pl.program_id(1), q_ref[...], k_ref, v_ref)
     o_ref[...] = out
     low_ref[...] = out.astype(bf)
-    logs = jnp.concatenate([peak0 + jnp.log2(total0), peak1 + jnp.log2(total1)], axis=0)
     l_ref[...] = logs.reshape(1, 2, BLOCK)
 
 
@@ -1054,25 +1037,13 @@
     )(queries, keys, values)
 
 
-def attend_back_kernel(
-    q_ref, k_ref, v_ref, g_ref, a_ref, l_ref, cq_ref, sq_ref, c_ref, s_ref,
-    dq_ref, dk_ref, dv_ref, dk, dv,
-):
-    i = pl.program_id(1)
-
-    @pl.when(i == 0)
-    def _():
-        dk[...] = jnp.zeros_like(dk)
-        dv[...] = jnp.zeros_like(dv)
-
-    queries, grads = q_ref[...], g_ref[...]
+def attend_back_rows(i, queries, grads, attended, logs, k_ref, v_ref, dk, dv):
     heads = [one_head(queries, h) for h in range(2)]
     grad_heads = [one_head(grads, h) for h in range(2)]
     both_heads = jnp.concatenate(heads, axis=0)
     both_grads = jnp.concatenate(grad_heads, axis=0)
-    products = (a_ref[...] * grads.astype(f32)).T
+    products = (attended * grads.astype(f32)).T
     dots = [jnp.sum(products[64 * h : 64 * h + 64], axis=0, keepdims=True) for h in range(2)]
-    logs = l_ref[0]
 
     def block(j, sums, masked):
         at = pl.ds(pl.multiple_of(j * BLOCK, BLOCK), BLOCK)
@@ -1102,20 +1073,42 @@
     sums = lax.fori_loop(0, i, lambda j, sums: block(j, sums, False), (zero, zero))
     sums = block(i, sums, True)
     lane = lax.broadcasted_iota(jnp.int32, zero.shape, 1)
-    query_grad = jnp.where(lane < 64, sums[0], sums[1]) * SCALE
-    dq_ref[...] = (query_grad * cq_ref[...] - partner(query_grad) * sq_ref[...]).astype(bf)
+    return jnp.where(lane < 64, sums[0], sums[1]) * SCALE
+
+
+def turn_back(grads, cosine, sine):
+    return (grads * cosine - partner(grads) * sine).astype(bf)
+
+
+def finish_keys(dk, dv, c_ref, s_ref, dk_ref, dv_ref):
+    def turn(t, _):
+        at = pl.ds(pl.multiple_of(t * 256, 256), 256)
+        dk_ref[at, :] = turn_back(dk[at, :] * SCALE, c_ref[at, :], s_ref[at, :])
+        dv_ref[at, :] = dv[at, :].astype(bf)
+        return 0
+
+    lax.fori_loop(0, dk.shape[0] // 256, turn, 0)
+
+
+def attend_back_kernel(
+    q_ref, k_ref, v_ref, g_ref, a_ref, l_ref, cq_ref, sq_ref, c_ref, s_ref,
+    dq_ref, dk_ref, dv_ref, dk, dv,
+):
+    i = pl.program_id(1)
+
+    @pl.when(i == 0)
+    def _():
+        dk[...] = jnp.zeros_like(dk)
+        dv[...] = jnp.zeros_like(dv)
+
+    query_grad = attend_back_rows(
+        i, q_ref[...], g_ref[...], a_ref[...], l_ref[0], k_ref, v_ref, dk, dv
+    )
+    dq_ref[...] = turn_back(query_grad, cq_ref[...], sq_ref[...])
 
     @pl.when(i == pl.num_programs(1) - 1)
     def _():
-        def turn(t, _):
-            at = pl.ds(pl.multiple_of(t * 256, 256), 256)
-            key_grad = dk[at, :] * SCALE
-            turned = key_grad * c_ref[at, :] - partner(key_grad) * s_ref[at, :]
-            dk_ref[at, :] = turned.astype(bf)
-            dv_ref[at, :] = dv[at, :].astype(bf)
-            return 0
-
-        lax.fori_loop(0, dk.shape[0] // 256, turn, 0)
+        finish_keys(dk, dv, c_ref, s_ref, dk_ref, dv_ref)
 
 
 def attend_back(queries, keys, values, grads, attended, logs, cosine, sine):
@@ -1134,6 +1127,437 @@
         scratch_shapes=[pltpu.VMEM((tokens, 128), f32), pltpu.VMEM((tokens, 128), f32)],
         compiler_params=params_for(),
     )(queries, keys, values, grads, attended, logs, cosine, sine, cosine, sine)
+
+
+def swap_copies(take, put, ss, rs, base):
+    z, x, y, c = coords()
+    others = [(y, 1 - c), (1 - y, c), (1 - y, 1 - c)]
+    me = y * 2 + c
+    starts, arrivals = [], []
+    for i, (yy, cc) in enumerate(others):
+        starts.append(
+            remote(take(yy * 2 + cc), put(me), ss.at[base + i], rs.at[base + i], dev(z, x, yy, cc))
+        )
+        ref = put(yy * 2 + cc)
+        arrivals.append(remote(ref, ref, ss.at[base + i], rs.at[base + i], dev(z, x, yy, cc)))
+    return me, starts, arrivals
+
+
+def forward_kernel(
+    h_ref, n_ref, w_ref, cos_ref, sin_ref, can_ref,
+    g_ref, normed_ref, q_ref, k_ref, v_ref, o_ref, l_ref, t_ref,
+    low, ss, rs, ls, ts, tr,
+):
+    z, x, y, c = coords()
+    pump, steps, finish = gather_steps(
+        can_ref, g_ref, ss, rs, ls, [dev(z, x, 1 - y, 1 - c)]
+    )
+    pump(0, 0)
+    pump(1, 0)
+
+    def project_step(t, _):
+        at = pl.ds(pl.multiple_of(t * 256, 256), 256)
+        parts = project_rows(h_ref[at, :], n_ref, w_ref, cos_ref[at, :], sin_ref[at, :])
+        for ref, part in zip((normed_ref, q_ref, k_ref, v_ref), parts):
+            ref[at, :] = part
+
+        @pl.when(lax.rem(t, 4) == 3)
+        def _():
+            pump(2 + t // 4, 0)
+
+        return 0
+
+    lax.fori_loop(0, 8, project_step, 0)
+
+    def attend_step(t, _):
+        p = t // 4
+        i = t - 4 * p
+        at = pl.ds(pl.multiple_of(i * BLOCK, BLOCK), BLOCK)
+        lanes = pl.ds(pl.multiple_of(p * 128, 128), 128)
+        out, logs = attend_rows(i, q_ref[at, lanes], k_ref.at[:, lanes], v_ref.at[:, lanes])
+        o_ref[at, lanes] = out
+        low[at, lanes] = out.astype(bf)
+        l_ref[p, :, at] = logs
+        pump(4 + t, 0)
+        return 0
+
+    lax.fori_loop(0, 8, attend_step, 0)
+
+    def take(owner):
+        return low.at[pl.ds(pl.multiple_of(owner * 512, 512), 512)]
+
+    def put(owner):
+        return t_ref.at[:, pl.ds(pl.multiple_of(owner * 256, 256), 256)]
+
+    me, starts, arrivals = swap_copies(take, put, ts, tr, 0)
+    for copy in starts:
+        copy.start()
+    own = pltpu.make_async_copy(take(me), put(me), ts.at[3])
+    own.start()
+    lax.fori_loop(12, steps, pump, 0)
+    for copy in arrivals:
+        copy.wait_recv()
+    for copy in starts:
+        copy.wait_send()
+    own.wait()
+    finish()
+
+
+def forward(hidden, norm_rows, w_qkv, cosine, sine, canonical):
+    shape = jax.ShapeDtypeStruct
+    return pl.pallas_call(
+        forward_kernel,
+        out_shape=(
+            shape((24 * SHARD, D), bf), shape((2048, D), bf),
+            shape((2048, 256), bf), shape((2048, 256), bf), shape((2048, 256), bf),
+            shape((2048, 256), f32), shape((2, 2, 2048), f32), shape((512, D), bf),
+        ),
+        in_specs=[VM] * 6,
+        out_specs=(ANY,) + (VM,) * 7,
+        scratch_shapes=[
+            pltpu.VMEM((2048, 256), bf),
+            DMA((11, UNITS)), DMA((11, UNITS)), DMA, DMA((4,)), DMA((3,)),
+        ],
+        compiler_params=params_for(1),
+    )(hidden, norm_rows, w_qkv, cosine, sine, canonical)
+
+
+def backward_kernel(
+    gw_ref, ag_ref, q_ref, k_ref, v_ref, a_ref, l_ref, cos_ref, sin_ref,
+    own_ref, dq_ref, dk_ref, dv_ref,
+    grads, dk, dv, ts, tr, *rooms,
+):
+    z, x, y, c = coords()
+    pump, steps, finish = reduce_steps(gw_ref, own_ref, *rooms, [dev(z, x, 1 - y, 1 - c)])
+
+    def take(owner):
+        return ag_ref.at[:, pl.ds(pl.multiple_of(owner * 256, 256), 256)]
+
+    def put(owner):
+        return grads.at[pl.ds(pl.multiple_of(owner * 512, 512), 512)]
+
+    me, starts, arrivals = swap_copies(take, put, ts, tr, 0)
+    for copy in starts:
+        copy.start()
+    own = pltpu.make_async_copy(take(me), put(me), ts.at[3])
+    own.start()
+    pump(0, 0)
+    pump(1, 0)
+    for copy in arrivals:
+        copy.wait_recv()
+    own.wait()
+
+    def step(t, _):
+        p = t // 4
+        i = t - 4 * p
+        at = pl.ds(pl.multiple_of(i * BLOCK, BLOCK), BLOCK)
+        lanes = pl.ds(pl.multiple_of(p * 128, 128), 128)
+
+        @pl.when(i == 0)
+        def _():
+            dk[...] = jnp.zeros_like(dk)
+            dv[...] = jnp.zeros_like(dv)
+
+        query_grad = attend_back_rows(
+            i, q_ref[at, lanes], grads[at, lanes], a_ref[at, lanes], l_ref[p, :, at],
+            k_ref.at[:, lanes], v_ref.at[:, lanes], dk, dv,
+        )
+        dq_ref[at, lanes] = turn_back(query_grad, cos_ref[at, :], sin_ref[at, :])
+
+        @pl.when(i == 3)
+        def _():
+            finish_keys(
+                dk, dv, cos_ref, sin_ref, dk_ref.at[:, lanes], dv_ref.at[:, lanes]
+            )
+
+        pump(2 + t, 0)
+        return 0
+
+    lax.fori_loop(0, 8, step, 0)
+    lax.fori_loop(10, steps, pump, 0)
+    for copy in starts:
+        copy.wait_send()
+    finish()
+
+
+def backward(weight_grads, attended_grad, queries, keys, values, attended, logs, cosine, sine):
+    shape = jax.ShapeDtypeStruct
+    room = pltpu.VMEM
+    return pl.pallas_call(
+        backward_kernel,
+        out_shape=(shape((SHARD, D), f32),) + (shape((2048, 256), bf),) * 3,
+        in_specs=[ANY] + [VM] * 8,
+        out_specs=(VM,) * 4,
+        scratch_shapes=[
+            room((2048, 256), bf), room((2048, 128), f32), room((2048, 128), f32),
+            DMA((4,)), DMA((3,)), *reduce_rooms(),
+        ],
+        compiler_params=params_for(2, 60),
+    )(weight_grads, attended_grad, queries, keys, values, attended, logs, cosine, sine)
+
+
+ROWS = 128
+GELU_A = math.sqrt(2.0 / math.pi)
+GELU_B = 0.044715
+
+
+def mean_of(values):
+    return jnp.mean(values, axis=-1, keepdims=True)
+
+
+def unit_of(values):
+    center = values - mean_of(values)
+    inverse = lax.rsqrt(mean_of(center * center) + EPSILON)
+    return center * inverse, inverse
+
+
+def into_norm(grads, unit, inverse, gain):
+    scaled = grads * gain
+    return inverse * (scaled - mean_of(scaled) - unit * mean_of(scaled * unit))
+
+
+def fold(values):
+    total = values[0:8]
+    for at in range(8, values.shape[0], 8):
+        total = total + values[at : at + 8]
+    return total
+
+
+def up_pieces(j):
+    pieces = [(D + 32 * j, 0, 32)]
+    pieces += [(D + 128 + 384 * i + 96 * j, 32 + 96 * i, 96) for i in range(10)]
+    pieces.append((D + 3968 + 32 * j, 992, 32))
+    return pieces
+
+
+def dense_kernel(
+    a_ref, h_ref, c_ref, scale_ref, n_ref, w_ref,
+    o_ref, rg_ref, ag_ref, gw_ref, ns_ref, sq_ref,
+    wo, wu, wd, residual, branch, lowered, entered, act, slope, lgrad, egrad, stage, sums,
+    ws, ups, gs,
+):
+    tokens = a_ref.shape[0]
+    pieces = tokens // ROWS
+    load_o = pltpu.make_async_copy(w_ref.at[0:D], wo, ws.at[0])
+    loads_d = [
+        pltpu.make_async_copy(w_ref.at[5 * D + D * j : 6 * D + D * j], wd.at[j], ws.at[1 + j])
+        for j in range(4)
+    ]
+    loads_u = [
+        [
+            pltpu.make_async_copy(
+                w_ref.at[src : src + count], wu.at[j, to : to + count], ups.at[j, i]
+            )
+            for i, (src, to, count) in enumerate(up_pieces(j))
+        ]
+        for j in range(4)
+    ]
+    load_o.start()
+    for j in range(4):
+        for copy in loads_u[j]:
+            copy.start()
+    for copy in loads_d:
+        copy.start()
+    sums[...] = jnp.zeros_like(sums)
+    width = 1024
+
+    def columns(t):
+        return pl.ds(pl.multiple_of(t * width, width), width)
+
+    def over_columns(body, count=D // width):
+        def go(t, _):
+            body(columns(t))
+            return 0
+
+        lax.fori_loop(0, count, go, 0)
+
+    def over_rows(body):
+        def go(t, _):
+            body(pl.ds(pl.multiple_of(t * ROWS, ROWS), ROWS))
+            return 0
+
+        lax.fori_loop(0, pieces, go, 0)
+
+    load_o.wait()
+
+    def branch_step(at):
+        branch[:, at] = jnp.dot(a_ref[...], wo[:, at], preferred_element_type=f32)
+
+    over_columns(branch_step)
+
+    def enter_step(at):
+        values = branch[at, :]
+        unit, _ = unit_of(values)
+        res = h_ref[at, :].astype(f32) + unit * n_ref[2:3, :] + n_ref[3:4, :]
+        residual[at, :] = res
+        unit, _ = unit_of(res)
+        entered[at, :] = (unit * n_ref[4:5, :] + n_ref[5:6, :]).astype(bf)
+        sums[0] += fold(values * values)
+
+    over_rows(enter_step)
+
+    for j in range(4):
+        for copy in loads_u[j]:
+            copy.wait()
+
+        def lift_step(at):
+            lifted = jnp.dot(entered[...], wu[j, :, at], preferred_element_type=f32)
+            square = lifted * lifted
+            tanh = jnp.tanh(lifted * (GELU_A + (GELU_A * GELU_B) * square))
+            half = 0.5 + 0.5 * tanh
+            act[j, :, at] = (lifted * half).astype(bf)
+            slope[j, :, at] = half + lifted * (0.5 - 0.5 * tanh * tanh) * (
+                GELU_A + (3.0 * GELU_A * GELU_B) * square
+            )
+
+        over_columns(lift_step)
+    for copy in loads_d:
+        copy.wait()
+
+    def lower_step(at):
+        total = jnp.dot(act[0], wd[0, :, at], preferred_element_type=f32)
+        for j in range(1, 4):
+            total = total + jnp.dot(act[j], wd[j, :, at], preferred_element_type=f32)
+        lowered[:, at] = total
+
+    over_columns(lower_step)
+    scale = scale_ref[0, 0]
+
+    def out_step(at):
+        values = lowered[at, :]
+        unit, inverse = unit_of(values)
+        o_ref[at, :] = (residual[at, :] + unit * n_ref[6:7, :] + n_ref[7:8, :]).astype(bf)
+        upstream = c_ref[at, :].astype(f32) * scale
+        lgrad[at, :] = into_norm(upstream, unit, inverse, n_ref[6:7, :]).astype(bf)
+        sums[1] += fold(values * values)
+        sums[2] += fold(upstream * unit)
+        sums[3] += fold(upstream)
+
+    over_rows(out_step)
+
+    def store(buffer, j, slot):
+        return [
+            pltpu.make_async_copy(
+                stage.at[buffer, to : to + count], gw_ref.at[src : src + count], gs.at[slot, i]
+            )
+            for i, (src, to, count) in enumerate(up_pieces(j))
+        ]
+
+    def store_block(buffer, first, slot):
+        return [pltpu.make_async_copy(stage.at[buffer], gw_ref.at[first : first + D], gs.at[slot, 0])]
+
+    pending = {}
+
+    def reuse(buffer):
+        for copy in pending.pop(buffer, []):
+            copy.wait()
+
+    def issue(buffer, copies):
+        for copy in copies:
+            copy.start()
+        pending[buffer] = copies
+
+    for j in range(4):
+        reuse(0)
+
+        def down_step(at):
+            stage[0, at, :] = lax.dot_general(
+                act[j, :, at], lgrad[...], TN, preferred_element_type=f32
+            ).astype(bf)
+
+        over_columns(down_step)
+        issue(0, store_block(0, 5 * D + D * j, 0))
+
+        def slope_step(at):
+            grads = lax.dot_general(lgrad[...], wd[j, at, :], NT, preferred_element_type=f32)
+            act[j, :, at] = (grads * slope[j, :, at]).astype(bf)
+
+        over_columns(slope_step)
+        reuse(1)
+
+        def up_step(at):
+            stage[1, :, at] = lax.dot_general(
+                entered[...], act[j, :, at], TN, preferred_element_type=f32
+            ).astype(bf)
+
+        over_columns(up_step)
+        issue(1, store(1, j, 1))
+
+    def enter_back_step(at):
+        total = lax.dot_general(act[0], wu[0, at, :], NT, preferred_element_type=f32)
+        for j in range(1, 4):
+            total = total + lax.dot_general(act[j], wu[j, at, :], NT, preferred_element_type=f32)
+        egrad[:, at] = total
+
+    over_columns(enter_back_step)
+
+    def branch_back_step(at):
+        grads = egrad[at, :]
+        upstream = c_ref[at, :].astype(f32) * scale
+        unit, inverse = unit_of(residual[at, :])
+        res_grad = upstream + into_norm(grads, unit, inverse, n_ref[4:5, :])
+        rg_ref[at, :] = res_grad
+        sums[4] += fold(grads * unit)
+        sums[5] += fold(grads)
+        unit, inverse = unit_of(branch[at, :])
+        lgrad[at, :] = into_norm(res_grad, unit, inverse, n_ref[2:3, :]).astype(bf)
+        sums[6] += fold(res_grad * unit)
+        sums[7] += fold(res_grad)
+
+    over_rows(branch_back_step)
+    reuse(0)
+
+    def out_grad_step(at):
+        stage[0, at, :] = lax.dot_general(
+            a_ref[:, at], lgrad[...], TN, preferred_element_type=f32
+        ).astype(bf)
+
+    over_columns(out_grad_step)
+    issue(0, store_block(0, 0, 0))
+
+    def attended_step(at):
+        ag_ref[:, at] = lax.dot_general(
+            lgrad[...], wo[at, :], NT, preferred_element_type=f32
+        ).astype(bf)
+
+    over_columns(attended_step)
+    order = [None, None, 6, 7, 4, 5, 2, 3]
+    for row, source in enumerate(order):
+        if source is None:
+            ns_ref[row : row + 1, :] = jnp.zeros((1, D), f32)
+        else:
+            ns_ref[row : row + 1, :] = jnp.sum(sums[source], axis=0, keepdims=True)
+    lane = lax.broadcasted_iota(jnp.int32, (8, 128), 1)
+    row = lax.broadcasted_iota(jnp.int32, (8, 128), 0)
+    told = jnp.zeros((8, 128), f32)
+    for t in range(2):
+        told = jnp.where((lane == t) & (row == 0), jnp.sum(sums[t]), told)
+    sq_ref[...] = told
+    reuse(0)
+    reuse(1)
+
+
+def dense(attended, hidden, cotangent, scale, norm_rows, weights):
+    tokens = attended.shape[0]
+    shape = jax.ShapeDtypeStruct
+    room = pltpu.VMEM
+    return pl.pallas_call(
+        dense_kernel,
+        out_shape=(
+            shape((tokens, D), bf), shape((tokens, D), f32), shape((tokens, D), bf),
+            shape((9 * D, D), bf), shape((8, D), f32), shape((8, 128), f32),
+        ),
+        in_specs=[VM, VM, VM, pl.BlockSpec(memory_space=pltpu.SMEM), VM, ANY],
+        out_specs=(VM, VM, VM, ANY, VM, VM),
+        scratch_shapes=[
+            room((D, D), bf), room((4, D, D), bf), room((4, D, D), bf),
+            room((tokens, D), f32), room((tokens, D), f32), room((tokens, D), f32),
+            room((tokens, D), bf), room((4, tokens, D), bf), room((4, tokens, D), f32),
+            room((tokens, D), bf), room((tokens, D), f32), room((2, D, D), bf),
+            room((8, 8, D), f32), DMA((5,)), DMA((4, 12)), DMA((2, 12)),
+        ],
+        compiler_params=params_for(mib=60),
+    )(attended, hidden, cotangent, scale, norm_rows, weights)
 
 
 def norm_forward(values, gain_row, shift_row):
@@ -1197,7 +1621,9 @@
         w_qkv = lax.dynamic_index_in_dim(
             parts[0].reshape(D, 3, width, D // width).transpose(1, 2, 0, 3), place, 1, False
         )
-        w_out, w_up, w_down = parts[1].reshape(D, D), parts[2].reshape(D, FF), parts[3].reshape(FF, D)
+        others = jnp.concatenate(
+            [parts[1].reshape(D, D), up_to_shards(parts[2].reshape(D, FF)), parts[3].reshape(FF, D)]
+        )
         norm_rows = whole[ends[-1] :].reshape(8, D).astype(f32)
         hidden_all = lax.all_gather(hidden, "fsdp", axis=0, tiled=True)
         places = lax.all_gather(positions[0].astype(f32), "fsdp", axis=0, tiled=True)
@@ -1207,83 +1633,54 @@
     angles = places[:, None] * frequency
     cosine = jnp.cos(angles)
     sine = jnp.where(lane < 32, -1.0, 1.0) * jnp.sin(angles)
-    normed_all, queries, keys, values = project(hidden_all, norm_rows, w_qkv, cosine, sine)
-    attended_all, attended_low, logs = attend(queries, keys, values)
-    attended = swap(attended_low, width, True, 4)
     if lines:
-        others = gather_others(canonical)
-        w_out, w_up, w_down = others[:D], up_from_shards(others[D : 5 * D]), others[5 * D :]
-
-    inputs = hidden.astype(f32)
-    branch = dots(attended, w_out, (1, 0))
-    branch_norm, branch_unit, branch_inverse = norm_forward(branch, norm_rows[2], norm_rows[3])
-    residual = inputs + branch_norm
-    entered, entered_unit, entered_inverse = norm_forward(residual, norm_rows[4], norm_rows[5])
-    entered_low = entered.astype(bf)
-    lifted = dots(entered_low, w_up, (1, 0))
-    activated = jax.nn.gelu(lifted).astype(bf)
-    lowered = dots(activated, w_down, (1, 0))
-    lowered_norm, lowered_unit, lowered_inverse = norm_forward(lowered, norm_rows[6], norm_rows[7])
-    output = (residual + lowered_norm).astype(bf)
-    squares = jnp.stack([jnp.mean(branch * branch), jnp.mean(lowered * lowered)])
-
+        others, normed_all, queries, keys, values, attended_all, logs, attended = forward(
+            hidden_all, norm_rows, w_qkv, cosine, sine, canonical
+        )
+    else:
+        normed_all, queries, keys, values = project(hidden_all, norm_rows, w_qkv, cosine, sine)
+        attended_all, attended_low, logs = attend(queries, keys, values)
+        attended = swap(attended_low, width, True, 4)
     source_table = jnp.arange(corpus_weight.shape[0], dtype=jnp.int32)
     row_scale = jnp.sum(jnp.where(source_ids[0] == source_table, corpus_weight, 0.0))
-    upstream = cotangent[0].astype(f32) * row_scale
-    lowered_grad = norm_backward(upstream, lowered_unit, lowered_inverse, norm_rows[6]).astype(bf)
-    grad_down = dots(activated, lowered_grad, (0, 0))
-    activated_grad = dots(lowered_grad, w_down, (1, 1))
-    lifted_grad = jax.vjp(jax.nn.gelu, lifted)[1](activated_grad)[0].astype(bf)
-    grad_up = dots(entered_low, lifted_grad, (0, 0))
-    entered_grad = dots(lifted_grad, w_up, (1, 1))
-    residual_grad = upstream + norm_backward(
-        entered_grad, entered_unit, entered_inverse, norm_rows[4]
+    output, residual_grad, attended_grad, weight_grads, norm_part, squares = dense(
+        attended, hidden, cotangent[0], row_scale.reshape(1, 1), norm_rows, others
     )
-    branch_grad = norm_backward(residual_grad, branch_unit, branch_inverse, norm_rows[2]).astype(bf)
-    grad_out = dots(attended, branch_grad, (0, 0))
-    attended_grad = dots(branch_grad, w_out, (1, 1)).astype(bf)
     if lines:
-        flat = jnp.concatenate(
-            [grad_out.astype(bf), up_to_shards(grad_up.astype(bf)), grad_down.astype(bf)], axis=0
+        owned, *mixed_grad = backward(
+            weight_grads, attended_grad, queries, keys, values, attended_all, logs, cosine, sine
         )
-        owned = reduce_others(flat)
-
-    grads_all = swap(attended_grad, width, False, 5)
-    mixed_grad = attend_back(
-        queries, keys, values, grads_all, attended_all, logs, cosine, sine
-    )
+    else:
+        grads_all = swap(attended_grad, width, False, 5)
+        mixed_grad = attend_back(
+            queries, keys, values, grads_all, attended_all, logs, cosine, sine
+        )
     grad_qkv = jnp.stack([dots(normed_all, part, (0, 0)) for part in mixed_grad])
     normed_part = sum(dots(part, w_qkv[j], (1, 1)) for j, part in enumerate(mixed_grad))
     _, unit_all, _ = norm_forward(hidden_all.astype(f32), norm_rows[0], norm_rows[1])
-    norm_part = jnp.stack(
-        [
-            *norm_sums(normed_part, unit_all),
-            *norm_sums(residual_grad, branch_unit),
-            *norm_sums(entered_grad, entered_unit),
-            *norm_sums(upstream, lowered_unit),
-        ]
-    )
+    norm_part = jnp.concatenate([jnp.stack(norm_sums(normed_part, unit_all)), norm_part[2:]], axis=0)
     if lines:
-        told = jnp.zeros((8, 128), f32).at[0, :2].set(squares)
-        param_grads, normed_grad, told = last_reduce(
-            grad_qkv.astype(bf), normed_part.astype(bf), owned, norm_part, told
+        param_grads, normed_grad, squares = last_reduce(
+            grad_qkv.astype(bf), normed_part.astype(bf), owned, norm_part, squares
         )
         param_grads = param_grads.reshape(-1)
-        squares = told[0, :2]
     else:
-        spread = jnp.zeros((3, width, D, D // width), f32)
-        spread = lax.dynamic_update_slice_in_dim(spread, grad_qkv[:, None], place, 1)
-        flat = jnp.concatenate(
-            [
-                part.reshape(-1)
-                for part in (spread.transpose(2, 0, 1, 3), grad_out, grad_up, grad_down, norm_part)
-            ]
+        spread = jnp.zeros((3, width, D, D // width), bf)
+        spread = lax.dynamic_update_slice_in_dim(spread, grad_qkv.astype(bf)[:, None], place, 1)
+        parts = (
+            spread.transpose(2, 0, 1, 3),
+            weight_grads[:D],
+            up_from_shards(weight_grads[D : 5 * D]),
+            weight_grads[5 * D :],
+            norm_part.astype(bf),
         )
+        flat = jnp.concatenate([part.reshape(-1) for part in parts])
         param_grads = lax.psum_scatter(flat, ("dp", "fsdp"), scatter_dimension=0, tiled=True)
+        param_grads = param_grads.astype(f32)
         normed_grad = lax.psum_scatter(normed_part, "fsdp", scatter_dimension=0, tiled=True)
         squares = lax.psum(squares, ("dp", "fsdp"))
-    statistics = squares / devices
-    _, normed_unit, normed_inverse = norm_forward(inputs, norm_rows[0], norm_rows[1])
+    statistics = squares[0, :2] / (devices * tokens * D)
+    _, normed_unit, normed_inverse = norm_forward(hidden.astype(f32), norm_rows[0], norm_rows[1])
     into_input = norm_backward(normed_grad, normed_unit, normed_inverse, norm_rows[0])
     input_grad = (residual_grad + into_input).astype(bf)
     return (output[None], input_grad[None], param_grads, statistics)

time: 602 us -> 440 us (0.73)
  local copies, waits for them, and re-layouts: 92.9 us -> 13.9 us
  matrix products: 79.9 us -> 18 us
  other arithmetic: 26.7 us -> 12.2 us
  Pallas kernels: 393 us -> 385 us
    dot_general x15 -> x6, matrix products: 79.9 us -> 18 us  [dots(): lax.dot_general(a, b, ((contract[:1], contract[1:]), ((), ())), preferred...]
    reshape x9 -> x0, local copies, waits for them, and re-layouts: 33.5 us -> none  [the longest x6 20.6 us: up_to_shards(): piece.reshape(blocks, rows, 4, D).transpose(0, 2, 1, 3).reshape(-1, D)]
    unnamed x69 -> x49, local copies, waits for them, and re-layouts: 43.8 us -> 13 us
    pallas_call x7 -> x3, Pallas kernels: 283 us -> 266 us  [the longest x1 112 us: forward(): pl.pallas_call(forward_kernel, out_shape=(shape((24 * SHARD, D), bf), sha...]
    slice x4 -> x1, local copies, waits for them, and re-layouts: 14.8 us -> 0.01 us  [per_device(): norm_part[2:]]
    pallas_call x1, Pallas kernels: 68.2 us -> 77.2 us  [last_reduce(): pl.pallas_call(last_kernel, out_shape=(shape((NATURAL, 128), f32), shape(...]
    reduce_sum x3 -> x0, other arithmetic: 8.81 us -> none  [norm_sums(): return (jnp.sum(grad_rows * unit_rows, axis=0), jnp.sum(grad_rows, axis=0))]
where the time goes in v2:
time: 440 us; the launch traced here: 431 us
  Pallas kernels  385 us (88%)
  matrix products  18 us (4%)
  local copies, waits for them, and re-layouts  13.9 us (3%)
  other arithmetic  12.2 us (3%)
    pallas_call x1, Pallas kernels, forward(): pl.pallas_call(forward_kernel, out_shape=(shape((24 * SHARD, D), bf), sha...  112 us
    pallas_call x1, Pallas kernels, backward(): pl.pallas_call(backward_kernel, out_shape=(shape((SHARD, D), f32),) + (sh...  102 us
    pallas_call x1, Pallas kernels, last_reduce(): pl.pallas_call(last_kernel, out_shape=(shape((NATURAL, 128), f32), shape(...  77.2 us
    pallas_call x1, Pallas kernels, dense(): pl.pallas_call(dense_kernel, out_shape=(shape((tokens, D), bf), shape((to...  52.5 us
    pallas_call x1, Pallas kernels, first_gather(): pl.pallas_call(first_kernel, out_shape=(shape((2048, D), bf), shape((3, D...  42 us
    dot_general x6, matrix products, dots(): lax.dot_general(a, b, ((contract[:1], contract[1:]), ((), ())), preferred...  18 us
    unnamed x49, local copies, waits for them, and re-layouts  13 us

profile of v2, /device:TPU:5, one launch (start us, length us, event | category | flops | bytes accessed | tf_op | source)
XLA Modules:
  0.0 431.4 jit_solution(11564121078908138082)
XLA Ops:
  0.6 0.7 convert_element_type.25
  1.3 0.0 copy-start.2
  1.3 1.2 copy-done.2
  2.6 1.1 copy-done.12
  3.7 42.0 %shard_map.93 = (bf16[2048,1024]{1,0:T(8,128)(2,1)S(1)}, bf16[3,1024,256]{2,1,0:T(8,128)(2,1)S(1)}, bf16[384,1024]{1,0:T(8,128)(2,1)S(1)}, f32[8,1024]{1,0:T(8,128)S(1)}, f32[4,8,128]{2,1,0:T(8,128)S(1)}) custom-call(bf16[3074,128]{1,0:T(8,128)(2,1)S(1)} %bitcast.50, bf16[512,1024]{1,0:T(8,128)(2,1)S(1)} %bitcast.48, f32[8,128]{1,0:T(8,128)S(1)} %pad.4.pos_ref), custom_call_target="tpu_custom_call" | custom-call | tf_op jit(solution)/shard_map/pallas_call | solution.py:287
  45.7 0.0 copy-start
  45.7 2.0 copy-done
  47.7 0.0 copy-start.5
  47.7 1.1 copy-done.5
  48.8 0.0 copy-start.13
  48.8 5.0 %fusion.18 = (f32[2048,128]{1,0:T(8,128)}, f32[2048,128]{1,0:T(8,128)S(1)}) fusion(f32[128]{0:T(128)S(1)} %get-tuple-element.64, f32[128]{0:T(128)S(1)} %get-tuple-element.65, f32[2048]{0:T(1024)S(1)} %bitcast.54), kind=kLoop, calls=%fused_computation.30 | loop fusion | flops 524288 | bytes 2106368 | tf_op jit(solution)/shard_map/mul | solution.py:1635
  53.8 0.0 copy-start.4
  53.8 111.6 %shard_map.94 = (bf16[9216,1024]{1,0:T(8,128)(2,1)}, bf16[2048,1024]{1,0:T(8,128)(2,1)}, bf16[2048,256]{1,0:T(8,128)(2,1)S(1)}, bf16[2048,256]{1,0:T(8,128)(2,1)...) custom-call(bf16[2048,1024]{1,0:T(8,128)(2,1)} %copy-done, ...), custom_call_target="tpu_custom_call" | custom-call | tf_op jit(solution)/shard_map/pallas_call | solution.py:1208
  165.4 0.0 copy-done.13
  165.4 0.0 copy-done.4
  165.4 0.0 copy-start.8
  165.5 0.9 copy-done.8
  166.4 1.0 copy-done.9
  167.4 1.0 copy-done.10
  168.4 1.0 copy-done.11
  169.4 0.6 copy-done.14
  170.7 0.0 copy-done.23
  170.7 0.6 fusion.31
  171.3 52.5 %shard_map.95 = (bf16[512,1024]{1,0:T(8,128)(2,1)}, f32[512,1024]{1,0:T(8,128)}, bf16[512,1024]{1,0:T(8,128)(2,1)}, bf16[9216,1024]{1,0:T(8,128)(2,1)}, f32[8,1024]{1,0:T(8,128)}, /*index=5*/f32[8,128]{1,0:T(8,128)}) custom-call(bf16[512,1024]{1,0:T(8,128)(2,1)} %copy-done.8, bf16[512,1024]{1,0:T(8,128)(2,1)} %bitcast.47, bf16[512,1024]{1,0:T(8,128)(2,1)} %bitcast.51, ...), custom_call_target="tpu_custom_call" | custom-call | tf_op jit(solution)/shard_map/pallas_call | solution.py:1544
  223.8 0.0 copy-start.6
  223.8 102.0 %shard_map.96 = (f32[384,1024]{1,0:T(8,128)}, bf16[2048,256]{1,0:T(8,128)(2,1)}, bf16[2048,256]{1,0:T(8,128)(2,1)}, bf16[2048,256]{1,0:T(8,128)(2,1)}) custom-call(bf16[9216,1024]{1,0:T(8,128)(2,1)} %get-tuple-element.40.gw_ref, bf16[512,1024]{1,0:T(8,128)(2,1)} %get-tuple-element.41.ag_ref, bf16[2048,256]{1,0:T(8,128)(2,1)} %copy-done.9, ...), custom_call_target="tpu_custom_call" | custom-call | tf_op jit(solution)/shard_map/pallas_call | solution.py:1286
  325.8 0.0 copy-done.6
  325.8 0.0 copy-start.19
  325.8 2.6 fusion.21
  328.4 0.0 copy-done.19
  328.4 0.0 copy-start.1
  328.4 4.5 %fusion.23 = f32[2048,1024]{1,0:T(8,128)} fusion(bf16[2048,256]{1,0:T(8,128)(2,1)S(1)} %copy-done.19, bf16[3,1024,256]{2,1,0:T(8,128)(2,1)S(1)} %copy-done.6), kind=kOutput, calls=%fused_computation.35 | convolution fusion | flops 1073741824 | bytes 9961472 | tf_op jit(solution)/shard_map/dot_general | solution.py:1602
  332.9 0.0 copy-done.1
  332.9 0.6 convert_reduce_fusion
  333.6 0.0 copy-start.20
  333.6 1.4 fusion.2
  335.0 0.0 copy-done.20
  335.0 0.0 copy-start.21
  335.0 0.0 copy-start.22
  335.0 6.9 %fusion.4 = (f32[1024]{0:T(1024)S(1)}, f32[1024]{0:T(1024)S(1)}, bf16[2048,1024]{1,0:T(8,128)(2,1)}) fusion(bf16[2048,1024]{1,0:T(8,128)(2,1)S(1)} %copy-done.1, f32[2048]{0:T(1024)S(1)} %add_rsqrt_fusion, f32[2048]{0:T(1024)S(1)} %broadcast_multiply_fusion, bf16[2048,256]{1,0:T(8,128)(2,1)S(1)} %copy-done.20, bf16[3,1024,256]{2,1,0:T(8,128)(2,1)S(1)} %copy-done.6, ...), kind=kOutput, calls=%fused_computation.6 | convolution fusion | flops 1092614144 | bytes 26763264 | tf_op jit(solution)/shard_map/dot_general | solution.py:1602
  342.0 0.0 copy-done.21
  342.0 0.0 copy-done.22
  342.0 0.0 copy-start.18
  342.0 1.3 fusion.15
  343.4 0.0 copy-done.18
  343.4 1.3 fusion.16
  344.7 1.3 fusion.17
  346.1 0.0 copy-start.7
  346.1 0.0 copy-start.15
  346.1 0.2 pad_maximum_fusion.v_ref
  346.3 1.2 copy-done.7
  347.5 0.0 copy-done.15
  347.5 77.2 %shard_map.97 = (f32[3074,128]{1,0:T(8,128)S(1)}, f32[512,1024]{1,0:T(8,128)}, f32[8,128]{1,0:T(8,128)S(1)}) custom-call(bf16[3,1024,256]{2,1,0:T(8,128)(2,1)S(1)} %pad_maximum_fusion.v_ref, bf16[2048,1024]{1,0:T(8,128)(2,1)} %get-tuple-element.60.n_ref, f32[384,1024]{1,0:T(8,128)S(1)} %copy-done.7, f32[8,1024]{1,0:T(8,128)S(1)} %pad_maximum_fusion.1.nrm_ref, ...), custom_call_target="tpu_custom_call" | custom-call | tf_op jit(solution)/shard_map/pallas_call | solution.py:853
  424.7 0.0 copy-start.16
  424.7 0.9 slice.26
  425.6 0.0 copy-done.3
  425.6 0.2 convert_reduce_fusion.1
  425.8 0.4 fusion.14
  426.2 0.0 copy-done.16
  426.3 0.8 multiply_reduce_fusion
  427.1 0.4 copy-done.17
  427.5 1.7 fusion.19
  429.2 0.5 multiply_bitcast_fusion
  429.8 1.2 copy.12
  (19 shorter events, 0.1 us)
Async XLA Ops:
  1.3 1.2 copy-start.2
  2.5 1.1 copy-start.12
  45.7 2.0 copy-start
  47.7 1.1 copy-start.5
  48.8 116.6 %copy-start.13 = (f32[8,1024]{1,0:T(8,128)}, f32[8,1024]{1,0:T(8,128)S(1)}, u32[]{:S(2)}) copy-start(f32[8,1024]{1,0:T(8,128)S(1)} %get-tuple-element.31.n_ref) | copy-start | bytes 98308
  53.8 111.6 %copy-start.4 = (f32[2048,128]{1,0:T(8,128)}, f32[2048,128]{1,0:T(8,128)S(1)}, u32[]{:S(2)}) copy-start(f32[2048,128]{1,0:T(8,128)S(1)} %get-tuple-element.62.cos_ref) | copy-start | bytes 3145732
  53.8 116.9 %copy-start.23 = (f32[16]{0:T(128)S(1)}, f32[16]{0:T(128)}, u32[]{:S(2)}) copy-start(f32[16]{0:T(128)} %param.10) | copy-start | bytes 196
  165.4 1.0 copy-start.8
  166.4 1.0 copy-start.9
  167.4 1.0 copy-start.10
  168.4 1.0 copy-start.11
  169.4 0.6 copy-start.14
  223.8 102.0 %copy-start.6 = (bf16[3,1024,256]{2,1,0:T(8,128)(2,1)S(1)}, bf16[3,1024,256]{2,1,0:T(8,128)(2,1)}, u32[]{:S(2)}) copy-start(bf16[3,1024,256]{2,1,0:T(8,128)(2,1)} %copy-done.5) | copy-start | bytes 4718596
  325.8 2.6 copy-start.19
  328.4 4.5 %copy-start.1 = (bf16[2048,1024]{1,0:T(8,128)(2,1)S(1)}, bf16[2048,1024]{1,0:T(8,128)(2,1)}, u32[]{:S(2)}) copy-start(bf16[2048,1024]{1,0:T(8,128)(2,1)} %copy-done) | copy-start | bytes 12582916
  333.6 1.4 copy-start.20
  335.0 6.9 %copy-start.21 = (f32[8,1024]{1,0:T(8,128)S(1)}, f32[8,1024]{1,0:T(8,128)}, u32[]{:S(2)}) copy-start(f32[8,1024]{1,0:T(8,128)} %get-tuple-element.51) | copy-start | bytes 98308
  335.0 7.0 %copy-start.22 = (bf16[2048,1024]{1,0:T(8,128)(2,1)S(1)}, bf16[2048,1024]{1,0:T(8,128)(2,1)}, u32[]{:S(2)}) copy-start(bf16[2048,1024]{1,0:T(8,128)(2,1)} %get-tuple-element.39) | copy-start | bytes 12582916
  342.0 1.4 copy-start.18
  346.1 1.4 copy-start.7
  346.1 1.4 copy-start.15
  347.5 78.1 %copy-start.3 = (bf16[1,512,1024]{2,1,0:T(8,128)(2,1)S(1)}, bf16[1,512,1024]{2,1,0:T(8,128)(2,1)}, u32[]{:S(2)}) copy-start(bf16[1,512,1024]{2,1,0:T(8,128)(2,1)} %param.6) | copy-start | bytes 3145732
  424.7 1.6 copy-start.16
  425.8 1.7 copy-start.17
